TPU v7x, 256 devices: a whole 4x4x8 slice. The times are simulated.
256 devices in a mesh: dp: 16 (over x, y_lo, core), seq: 16 (over y_hi, z).
Axes of the slice: x: 4, y: 4 (y_hi: 2, y_lo: 2; y = y_hi * 2 + y_lo), z: 8, core: 2. Of those that a mesh axis runs over, the one named last changes fastest.
Arguments:
- dna_features: bfloat16 [16, 8192, 768], P('dp', 'seq'), may hold values from -6 to 6
- conv_weight: bfloat16 [5, 768, 1536], P(None, 'dp'), may hold values from -0.09375 to 0.09375
- conv_bias: float32 [1536], replicated, may hold values from -3 to 3
- norm_gain: float32 [1536], replicated, may hold values from 0.1 to 1.9
- query_weight: bfloat16 [1536, 1024], P('dp'), may hold values from -0.15625 to 0.15625
- kv_weight: bfloat16 [1536, 256], P('dp'), may hold values from -0.15625 to 0.15625
- out_weight: bfloat16 [1024, 1536], P('dp'), may hold values from -0.1875 to 0.1875
- head_scale: float32 [8], replicated, may hold values from 1.5 to 64
Outputs:
- tokens: bfloat16 [16, 4096, 1536], P('dp', 'seq')
- encoded: bfloat16 [16, 4096, 1536], P('dp', 'seq')
All inputs are finite; a program needn't handle non-finite values.
Results may differ from a plain program's by a relative error of at most 0.0095.
The roundings to bfloat16 on the way count: a program that leaves them out, or rounds other values in their place, can miss the bound.
Values may be sent and summed in bfloat16 or wider, within the bound.
No kernel may reach another device: no remote copies, remote signals or barrier semaphores. Data moves between devices by JAX's collectives and lax.ppermute only.
A program may use at most 128 MiB of HBM per device.

v0:
```python
import math

import jax
import jax.numpy as jnp
from jax import lax
from jax.sharding import PartitionSpec as P

C = 1536
HEADS = 8
HEAD_SIZE = 128
KW = 5
QW = 1024


def padded_2(shard, sides, width):
    for axis, dim in sides:
        peers, length = (lax.axis_size(axis), shard.shape[dim])
        up = [(i, (i + 1) % peers) for i in range(peers - 1)]
        down = [(j, i) for i, j in up]
        last = lax.slice_in_dim(shard, length - width, length, axis=dim)
        initial = lax.slice_in_dim(shard, 0, width, axis=dim)
        before = lax.ppermute(last, axis, up)
        after = lax.ppermute(initial, axis, down)
        shard = jnp.concatenate([before, shard, after], axis=dim)
    return shard


def on_device(
    dna_features, conv_weight, conv_bias, norm_gain, query_weight, kv_weight, out_weight, head_scale
):
    seq_rows = dna_features.shape[0]
    positions = dna_features.shape[1]
    margin = KW // 2
    padded = padded_2(dna_features, (("seq", 1),), margin)
    running = jnp.zeros((seq_rows, positions, C), jnp.float32)
    sequence_slice = lax.all_gather(conv_weight, "dp", axis=1, tiled=True)
    inputs = padded
    for kernel_tap in range(KW):
        running = running + jnp.einsum(
            "bpc,cf->bpf",
            inputs[:, kernel_tap : kernel_tap + positions],
            sequence_slice[kernel_tap],
            preferred_element_type=jnp.float32,
        )
    activated = jax.nn.gelu(running + conv_bias)
    tok_rows = positions // 2
    tokens = jnp.max(activated.reshape(seq_rows, tok_rows, 2, C), axis=2).astype(jnp.bfloat16)
    wide = tokens.astype(jnp.float32)
    stat = jnp.mean(jnp.square(wide), axis=-1, keepdims=True)
    normed = (wide * lax.rsqrt(stat + 1e-06) * norm_gain).astype(jnp.bfloat16)

    def project_rows(sequence_slice):
        return jnp.einsum("btc,cf->btf", normed, sequence_slice, preferred_element_type=jnp.float32)

    query_sum = project_rows(lax.all_gather(query_weight, "dp", axis=0, tiled=True))
    pair_sum = project_rows(lax.all_gather(kv_weight, "dp", axis=0, tiled=True))
    query_matrix = query_sum.astype(jnp.bfloat16).reshape(seq_rows, tok_rows, HEADS, HEAD_SIZE)
    pairs = pair_sum.astype(jnp.bfloat16)
    score_scale = head_scale / math.sqrt(HEAD_SIZE)
    sequence_slice = lax.all_gather(pairs, "seq", axis=1, tiled=True)
    top_old = jnp.full((seq_rows, HEADS, tok_rows), -jnp.inf, jnp.float32)
    totals_old = jnp.zeros((seq_rows, HEADS, tok_rows), jnp.float32)
    summed_old = jnp.zeros((seq_rows, HEADS, tok_rows, HEAD_SIZE), jnp.float32)
    scores = jnp.einsum(
        "eygl,ewl->egyw",
        query_matrix,
        sequence_slice[..., :HEAD_SIZE],
        preferred_element_type=jnp.float32,
    )
    scores = scores * score_scale[None, :, None, None]
    top_new = jnp.max(scores, axis=-1)
    correction_scale = jnp.exp(top_old - top_new)
    weights = jnp.exp(scores - top_new[..., None])
    fresh_totals = totals_old * correction_scale + jnp.sum(weights, axis=-1)
    summed_new = summed_old * correction_scale[..., None] + jnp.einsum(
        "wfpm,wmn->wfpn",
        weights.astype(jnp.bfloat16),
        sequence_slice[..., HEAD_SIZE:],
        preferred_element_type=jnp.float32,
    )
    context = summed_new / fresh_totals[..., None]
    context = (
        jnp.transpose(context, (0, 2, 1, 3)).reshape(seq_rows, tok_rows, QW).astype(jnp.bfloat16)
    )
    inputs = context
    update = jnp.einsum(
        "btc,cf->btf",
        inputs,
        lax.all_gather(out_weight, "dp", axis=0, tiled=True),
        preferred_element_type=jnp.float32,
    )
    encoded = (update + wide).astype(jnp.bfloat16)
    return (tokens, encoded)


def solution(mesh):
    in_specs = (
        P("dp", "seq", None),
        P(None, "dp", None),
        P(),
        P(),
        P("dp", None),
        P("dp", None),
        P("dp", None),
        P(),
    )
    out_specs = (P("dp", "seq", None), P("dp", "seq", None))
    return jax.shard_map(
        on_device, mesh=mesh, in_specs=in_specs, out_specs=out_specs, check_vma=False
    )
```

profile of v0, /device:TPU:2, one launch (start us, length us, event | category | flops | bytes accessed | tf_op | source)
XLA Modules:
  0.0 271.4 jit_solution(4873001197702816857)
XLA Ops:
  7.2 0.0 copy-start.1
  7.2 0.0 all-gather.6.cloned.1.call-start
  7.2 0.7 all-gather.6.cloned.1.call-update
  7.9 0.0 all-gather.8.cloned.1.call-start
  8.0 0.7 all-gather.8.cloned.1.call-update
  8.7 0.0 all-gather.12.cloned.1.call-start
  8.7 0.7 fusion.43
  9.4 3.8 %collective-permute-start = (bf16[1,2,768]{2,1,0:T(2,128)(2,1)S(1)}, bf16[1,2,768]{2,1,0:T(2,128)(2,1)S(1)}, u32[]{:S(2)}, u32[]{:S(2)}) collective-permute-start(bf16[1,2,768]{2,1,0:T(2,128)(2,1)S(1)} %get-tuple-element.2), channel_id=1, source_target_pairs={{0,1},{1,2},{2,3},{3,4},{4,5},{5,6},{6,7},{7,8},{8,9},{9,10},{10,1... | collective-permute-start | bytes 9224 | tf_op jit(solution)/shard_map/ppermute | solution.py:22
  13.3 1.3 collective-permute-start.1
  14.6 23.9 %all_gather.16 = bf16[1536,256]{1,0:T(8,128)(2,1)} all-gather(bf16[96,256]{1,0:T(8,128)(2,1)} %param.13), channel_id=1, replica_groups=mesh['dp'=16,'seq'=16] {'dp'}, dimensions={0}, use_global_device_ids=true | all-gather | bytes 835584 | tf_op jit(solution)/shard_map/all_gather | solution.py:56
  38.4 1.2 constant_dynamic-update-slice_fusion.1
  39.6 0.0 collective-permute-done.1
  39.6 0.0 copy-start.3
  39.7 0.0 collective-permute-done
  39.7 44.2 %all-gather.6.cloned.1.call-done = bf16[5,768,1536]{2,1,0:T(8,128)(2,1)} async-done(((bf16[5,48,1536]{2,1,0:T(8,128)(2,1)}), bf16[5,768,1536]{2,1,0:T(8,128)(2,1)}) %all-gather.6.cloned.1.call-update) | async-done | bytes 11796496 | tf_op jit(solution)/shard_map/all_gather | solution.py:36
  83.9 0.0 copy-done.1
  83.9 0.0 copy-start.6
  83.9 3.2 %fusion.18 = f32[512,1536]{1,0:T(8,128)S(1)} fusion(bf16[5,768,1536]{2,1,0:T(8,128)(2,1)} %all-gather.6.cloned.1.call-done, bf16[1,512,768]{2,1,0:T(8,128)(2,1)S(1)} %copy-done.1, bf16[1,2,768]{2,1,0:T(2,128)(2,1)S(1)} %collective-permute-done), kind=kOutput, calls=%fused_computation.31 | convolution fusion | flops 1209532416 | bytes 6294528 | tf_op jit(solution)/shard_map/bpc,cf->bpf/dot_general | solution.py:39
  87.1 0.0 copy-done.3
  87.1 3.8 %fusion.17 = f32[512,1536]{1,0:T(8,128)S(1)} fusion(bf16[5,768,1536]{2,1,0:T(8,128)(2,1)} %all-gather.6.cloned.1.call-done, bf16[1,514,768]{2,1,0:T(8,128)(2,1)S(1)} %constant_dynamic-update-slice_fusion), kind=kOutput, calls=%fused_computation.27 | convolution fusion | flops 1207959552 | bytes 6291456 | tf_op jit(solution)/shard_map/bpc,cf->bpf/dot_general | solution.py:39
  90.9 0.0 copy-done.6
  90.9 1.4 convolution_add_fusion.2
  92.3 0.0 copy-start.4
  92.3 0.0 copy-start.7
  92.4 1.4 convolution_add_fusion.1
  93.8 0.0 copy-done.4
  93.8 0.0 copy-done.7
  93.8 2.2 fusion.14
  96.0 0.0 copy-start.8
  96.1 0.6 reshape.180
  96.7 0.0 copy-start.2
  96.7 0.0 copy-start.9
  96.7 4.5 %reduce_max.18 = bf16[256,1536]{1,0:T(8,128)(2,1)S(1)} reduce(bf16[256,2,1536]{2,1,0:T(2,128)(2,1)S(1)} %reshape.180, bf16[]{:T(256)} %constant.71), dimensions={1}, to_apply=%region_0.0 | reduce | flops 393216 | bytes 2359298 | tf_op jit(solution)/shard_map/reduce_max | solution.py:47
  101.2 0.0 copy-start
  101.2 0.2 fusion.19
  101.5 0.0 copy-done.8
  101.5 0.0 copy-done.2
  101.5 1.1 convolution_convert_fusion.1
  102.6 0.0 all-gather.12.cloned.1.call-update
  102.6 0.2 all-gather.10.cloned.1.call-start
  102.9 0.3 all-gather.10.cloned.1.call-update
  103.2 0.0 copy-done.9
  103.2 25.4 %all-gather.8.cloned.1.call-done = bf16[1536,1024]{1,0:T(8,128)(2,1)} async-done(((bf16[96,1024]{1,0:T(8,128)(2,1)}), bf16[1536,1024]{1,0:T(8,128)(2,1)}) %all-gather.8.cloned.1.call-update) | async-done | bytes 3145744 | tf_op jit(solution)/shard_map/all_gather | solution.py:55
  128.6 2.9 %fusion.25 = bf16[32,8,8,128]{3,2,1,0:T(8,128)(2,1)S(1)} fusion(bf16[1536,1024]{1,0:T(8,128)(2,1)} %all-gather.8.cloned.1.call-done, bf16[256,1536]{1,0:T(8,128)(2,1)S(1)} %reduce_max.18, f32[1536]{0:T(1024)S(1)} %copy-done.8, f32[256]{0:T(256)S(1)} %add_rsqrt_fusion), kind=kOutput, calls=%fused_computation.38 | convolution fusion | flops 807141376 | bytes 4463616 | tf_op jit(solution)/shard_map/btc,cf->btf/dot_general | solution.py:53
  131.6 86.3 %all-gather.12.cloned.1.call-done = bf16[4096,256]{1,0:T(8,128)(2,1)} async-done(((bf16[256,256]{1,0:T(8,128)(2,1)}), bf16[4096,256]{1,0:T(8,128)(2,1)}) %all-gather.12.cloned.1.call-update) | async-done | bytes 2097168 | tf_op jit(solution)/shard_map/all_gather | solution.py:60
  217.8 14.5 %bitcast_reduce_fusion = (f32[8,256]{1,0:T(8,128)S(1)}, f32[4096,256,8]{1,0,2:T(8,128)}) fusion(f32[8]{0:T(128)S(1)} %broadcast_multiply_fusion, bf16[32,8,8,128]{3,2,1,0:T(8,128)(2,1)S(1)} %fusion.25, bf16[1,4096,256]{2,1,0:T(8,128)(2,1)} %bitcast.104), kind=kOutput, calls=%fused_computation.1 | convolution fusion | flops 2164258816 | bytes 35135520 | tf_op jit(solution)/shard_map/eygl,ewl->egyw/dot_general | solution.py:64
  232.3 0.0 copy-start.5
  232.3 14.6 %fusion.1 = f32[8,256]{1,0:T(8,128)S(1)} fusion(f32[4096,256,8]{1,0,2:T(8,128)} %get-tuple-element.7, f32[8,256]{1,0:T(8,128)S(1)} %get-tuple-element.6, f32[8]{0:T(128)S(1)} %broadcast_multiply_fusion), kind=kLoop, calls=%fused_computation.4 | loop fusion | flops 25163776 | bytes 33570848 | tf_op jit(solution)/shard_map/reduce_sum | solution.py:74
  247.0 0.0 copy-done.5
  247.0 14.1 %divide_convert_fusion = bf16[8,256,128]{1,2,0:T(8,128)(2,1)S(1)} fusion(bf16[1,4096,256]{2,1,0:T(8,128)(2,1)S(1)} %bitcast.105, f32[4096,256,8]{1,0,2:T(8,128)} %get-tuple-element.7, f32[8,256]{1,0:T(8,128)S(1)} %get-tuple-element.6, f32[8]{0:T(128)S(1)} %broadcast_multiply_fusion, f32[8,256]{1,0:T(8,128)S(1)} %get-tuple-element.5, ...), kind=kOutput, calls=%fused_computation.43 | convolution fusion | flops 2173435904 | bytes 35152384 | tf_op jit(solution)/shard_map/wfpm,wmn->wfpn/dot_general | solution.py:75
  261.1 0.0 all-gather.10.cloned.1.call-done
  261.1 0.0 copy-done
  261.1 3.8 %fusion.16 = bf16[1,256,1536]{2,1,0:T(8,128)(2,1)} fusion(bf16[256,1024]{0,1:T(8,128)(2,1)S(1)} %bitcast.106, bf16[1024,1536]{1,0:T(8,128)(2,1)} %all-gather.10.cloned.1.call-done, bf16[256,1536]{1,0:T(8,128)(2,1)S(1)} %reduce_max.18), kind=kOutput, calls=%fused_computation.23 | convolution fusion | flops 806486016 | bytes 5242880 | tf_op jit(solution)/shard_map/btc,cf->btf/dot_general | solution.py:86
  (4 shorter events, 0.0 us)
Async XLA Ops:
  7.2 76.7 %copy-start.1 = (bf16[1,512,768]{2,1,0:T(8,128)(2,1)S(1)}, bf16[1,512,768]{2,1,0:T(8,128)(2,1)}, u32[]{:S(2)}) copy-start(bf16[1,512,768]{2,1,0:T(8,128)(2,1)} %param.8) | copy-start | bytes 2359300
  7.2 76.7 %all-gather.6.cloned.1.call-start = ((), (), s32[]{:S(2)}) async-start(), calls=%async_computation | async-start | bytes 12533760 | tf_op jit(solution)/shard_map/all_gather | solution.py:36
  7.9 120.7 %all-gather.8.cloned.1.call-start = ((), (), s32[]{:S(2)}) async-start(), calls=%async_computation.1 | async-start | bytes 3342336 | tf_op jit(solution)/shard_map/all_gather | solution.py:55
  8.7 209.2 %all-gather.12.cloned.1.call-start = ((), (), s32[]{:S(2)}) async-start(), calls=%async_computation.3 | async-start | bytes 2228224 | tf_op jit(solution)/shard_map/all_gather | solution.py:60
  9.4 30.2 %collective-permute-start = (bf16[1,2,768]{2,1,0:T(2,128)(2,1)S(1)}, bf16[1,2,768]{2,1,0:T(2,128)(2,1)S(1)}, u32[]{:S(2)}, u32[]{:S(2)}) collective-permute-start(bf16[1,2,768]{2,1,0:T(2,128)(2,1)S(1)} %get-tuple-element.2), channel_id=1, source_target_pairs={{0,1},{1,2},{2,3},{3,4},{4,5},{5,6},{6,7},{7,8},{8,9},{9,10},{10,1... | collective-permute-start | bytes 9224 | tf_op jit(solution)/shard_map/ppermute | solution.py:22
  13.3 26.4 %collective-permute-start.1 = (bf16[1,2,768]{2,1,0:T(2,128)(2,1)S(1)}, bf16[1,2,768]{2,1,0:T(2,128)(2,1)S(1)}, u32[]{:S(2)}, u32[]{:S(2)}) collective-permute-start(bf16[1,2,768]{2,1,0:T(2,128)(2,1)S(1)} %get-tuple-element.3), channel_id=1, source_target_pairs={{1,0},{2,1},{3,2},{4,3},{5,4},{6,5},{7,6},{8,7},{9,8},{10,9},{11,1... | collective-permute-start | bytes 9224 | tf_op jit(solution)/shard_map/ppermute | solution.py:23
  39.6 47.5 %copy-start.3 = (bf16[1,514,768]{2,1,0:T(8,128)(2,1)}, bf16[1,514,768]{2,1,0:T(8,128)(2,1)S(1)}, u32[]{:S(2)}) copy-start(bf16[1,514,768]{2,1,0:T(8,128)(2,1)S(1)} %constant_dynamic-update-slice_fusion) | copy-start | bytes 2368516
  83.9 7.0 %copy-start.6 = (bf16[5,768,1536]{2,1,0:T(8,128)(2,1)S(1)}, bf16[5,768,1536]{2,1,0:T(8,128)(2,1)}, u32[]{:S(2)}) copy-start(bf16[5,768,1536]{2,1,0:T(8,128)(2,1)} %all-gather.6.cloned.1.call-done) | copy-start | bytes 35389444
  92.3 1.4 copy-start.4
  92.3 1.4 copy-start.7
  96.0 5.4 %copy-start.8 = (f32[1536]{0:T(1024)S(1)}, f32[1536]{0:T(1024)}, u32[]{:S(2)}) copy-start(f32[1536]{0:T(1024)} %param.11) | copy-start | bytes 18436
  96.7 4.8 %copy-start.2 = (bf16[1536,256]{1,0:T(8,128)(2,1)S(1)}, bf16[1536,256]{1,0:T(8,128)(2,1)}, u32[]{:S(2)}) copy-start(bf16[1536,256]{1,0:T(8,128)(2,1)} %all_gather.16) | copy-start | bytes 2359300
  96.7 6.5 %copy-start.9 = (f32[8]{0:T(128)S(1)}, f32[8]{0:T(128)}, u32[]{:S(2)}) copy-start(f32[8]{0:T(128)} %param.15) | copy-start | bytes 100
  101.2 159.9 %copy-start = (bf16[256,1536]{1,0:T(8,128)(2,1)}, bf16[256,1536]{1,0:T(8,128)(2,1)S(1)}, u32[]{:S(2)}) copy-start(bf16[256,1536]{1,0:T(8,128)(2,1)S(1)} %reduce_max.18) | copy-start | bytes 2359300
  102.6 158.5 %all-gather.10.cloned.1.call-start = ((), (), s32[]{:S(2)}) async-start(), calls=%async_computation.2 | async-start | bytes 3342336 | tf_op jit(solution)/shard_map/all_gather | solution.py:89
  232.3 14.6 %copy-start.5 = (bf16[4096,256]{1,0:T(8,128)(2,1)S(1)}, bf16[4096,256]{1,0:T(8,128)(2,1)}, u32[]{:S(2)}) copy-start(bf16[4096,256]{1,0:T(8,128)(2,1)} %all-gather.12.cloned.1.call-done) | copy-start | bytes 6291460
Sparse Core Ops, SparseCore 0:
  9.8 74.0 all-gather.5
  85.8 42.8 all-gather.7
  131.8 85.9 all-gather.11
  219.5 34.6 all-gather.9
where the time goes:
time: 272 us; the launch traced here: 271 us
  waiting for transfers between devices  158 us (58%)
  matrix products  48.4 us (18%)
  blocking collectives  23.9 us (9%)
  other arithmetic  19.4 us (7%)
  between operations  14 us (5%)
  starting transfers between devices  5.44 us (2%)
    all_gather x1, waiting for transfers between devices, on_device(): sequence_slice = lax.all_gather(pairs, 'seq', axis=1, tiled=True)  86.3 us
    all_gather x1, waiting for transfers between devices, on_device(): sequence_slice = lax.all_gather(conv_weight, 'dp', axis=1, tiled=True)  44.2 us
    all_gather x1, waiting for transfers between devices, on_device(): lax.all_gather(query_weight, 'dp', axis=0, tiled=True)  25.4 us
    all_gather x1, blocking collectives, on_device(): pair_sum = project_rows(lax.all_gather(kv_weight, 'dp', axis=0, tiled=True))  23.9 us
    reduce_sum x1, other arithmetic, on_device(): fresh_totals = totals_old * correction_scale + jnp.sum(weights, axis=-1)  14.6 us
    dot_general x1, matrix products, on_device(): jnp.einsum('eygl,ewl->egyw', query_matrix, sequence_slice[..., :HEAD_SIZE...  14.5 us
    dot_general x1, matrix products, on_device(): jnp.einsum('wfpm,wmn->wfpn', weights.astype(jnp.bfloat16), sequence_slice...  14.1 us
    dot_general x5, matrix products, on_device(): jnp.einsum('bpc,cf->bpf', inputs[:, kernel_tap:kernel_tap + positions], s...  12.1 us
  transfers between devices with their start and end apart: 6, of which 3 were waited for; matrix products, arithmetic and copies ran while one was open for 25% of the time, Pallas kernels for 0%

commit v1 on v0

v1 whole, which is shorter than its diff:
```python
import math

import jax
import jax.numpy as jnp
from jax import lax
from jax.experimental import pallas as pl
from jax.experimental.pallas import tpu as pltpu
from jax.sharding import PartitionSpec as P

CIN = 768
C = 1536
HEADS = 8
HEAD_SIZE = 128
KW = 5
QW = 1024
QUARTER = C // 4
TOKENS = 256
ROWS = CIN // 16
KV = 2 * HEAD_SIZE
REST = KV + QW + QW
BOTH = ("dp", "seq")
LOG2E = math.log2(math.e)
F32 = jnp.float32
BF16 = jnp.bfloat16


def places():
    for dp in range(16):
        for seq in range(16):
            yield dp // 4, dp // 2 % 2, dp % 2, seq // 8, seq % 8


def index(x, y_lo, core, y_hi, z):
    return (x * 4 + y_lo * 2 + core) * 16 + y_hi * 8 + z


def receive(value, source):
    pairs = [(index(*source(*p)), index(*p)) for p in places()]
    return lax.ppermute(value, BOTH, pairs)


def from_core(x, y, c, h, z):
    return x, y, 1 - c, h, z


def from_z_pair(x, y, c, h, z):
    return x, y, c, h, z ^ 1


def from_diagonal(x, y, c, h, z):
    return x, y, 1 - c, h, z ^ 1


def from_x(step):
    return lambda x, y, c, h, z: (x ^ step, y, c, h, z)


def from_y(step):
    def source(x, y, c, h, z):
        at = (h * 2 + y + step) % 4
        return x, at % 2, c, at // 2, z

    return source


def from_y_hi(x, y, c, h, z):
    return x, y, c, 1 - h, z


def from_z(step):
    return lambda x, y, c, h, z: (x, y, c, h, (z + step) % 8)


VMEM = pl.BlockSpec(memory_space=pltpu.VMEM)
SMEM = pl.BlockSpec(memory_space=pltpu.SMEM)
ANY = pl.BlockSpec(memory_space=pl.ANY)


def params(mib):
    return pltpu.CompilerParams(vmem_limit_bytes=mib * 2**20)


def run_copies(copies, sems):
    started = [pltpu.make_async_copy(a, b, sems.at[i]) for i, (a, b) in enumerate(copies)]
    for copy in started:
        copy.start()
    for copy in started:
        copy.wait()


UNITS = tuple(xr * 2 + yr for yr in (0, 1) for xr in (0, 1, 3, 2))


def conv_kernel(at_ref, a_ref, bias_ref, *refs):
    units, outs, (w_ref, sems) = refs[:8], refs[8:12], refs[12:]
    step = pl.program_id(0)

    @pl.when(step == 0)
    def _():
        copies = []
        for rel, unit in zip(UNITS, units):
            row = pl.multiple_of((at_ref[0] ^ rel) * (2 * ROWS), 2 * ROWS)
            copies.append((unit, w_ref.at[:, pl.ds(row, 2 * ROWS), :]))
        run_copies(copies, sems)

    w = w_ref[...].reshape(KW * CIN, QUARTER)
    bias = bias_ref[...]
    even = jnp.dot(a_ref[0, :, : KW * CIN], w, preferred_element_type=F32) + bias
    odd = jnp.dot(a_ref[0, :, CIN:], w, preferred_element_type=F32) + bias
    pooled = jnp.maximum(jax.nn.gelu(even), jax.nn.gelu(odd)).astype(BF16)
    for i, out in enumerate(outs):

        @pl.when(step == i)
        def _(out=out):
            out[...] = pooled


def convolve(chip, blocks, bias, units):
    return pl.pallas_call(
        conv_kernel,
        grid=(4,),
        out_shape=[jax.ShapeDtypeStruct((TOKENS, QUARTER), BF16)] * 4,
        in_specs=[SMEM, pl.BlockSpec((1, TOKENS, 6 * CIN), lambda i: (i, 0, 0)), VMEM] + [ANY] * 8,
        out_specs=[pl.BlockSpec((TOKENS, QUARTER), lambda i: (0, 0))] * 4,
        scratch_shapes=[pltpu.VMEM((KW, CIN, QUARTER), BF16), pltpu.SemaphoreType.DMA((8,))],
        compiler_params=params(40),
        cost_estimate=pl.CostEstimate(flops=6_040_000_000, bytes_accessed=14_000_000, transcendentals=786432),
    )(chip, blocks, bias, *units)


PACKED = tuple(
    (cr * 4 + yr * 2 + pair, slot, xr * 4 + yr * 2 + cr)
    for cr in (0, 1)
    for yr in (0, 1)
    for pair, xs in enumerate(((0, 1), (3, 2)))
    for slot, xr in enumerate(xs)
)


def norm_kernel(at_ref, *refs):
    parts, gain_ref, packed = refs[:4], refs[4], refs[5:13]
    tokens_ref, normed_ref, pairs_ref, w_ref, sems = refs[13:]
    copies = []
    for array, slot, rel in PACKED:
        row = pl.multiple_of((at_ref[0] ^ rel) * 96, 96)
        copies.append((packed[array].at[slot, :, pl.ds(0, KV)], w_ref.at[pl.ds(row, 96), :]))
    for i, part in enumerate(parts):
        column = pl.multiple_of((at_ref[1] ^ i) * QUARTER, QUARTER)
        tokens_ref[:, pl.ds(column, QUARTER)] = part[...]
    wide = tokens_ref[...].astype(F32)
    stat = jnp.mean(jnp.square(wide), axis=-1, keepdims=True)
    normed = (wide * lax.rsqrt(stat + 1e-06) * gain_ref[...]).astype(BF16)
    normed_ref[...] = normed
    run_copies(copies, sems)
    pairs_ref[...] = jnp.dot(normed, w_ref[...], preferred_element_type=F32).astype(BF16)


def norm_and_pairs(at, parts, gain, packed):
    return pl.pallas_call(
        norm_kernel,
        out_shape=[
            jax.ShapeDtypeStruct((TOKENS, C), BF16),
            jax.ShapeDtypeStruct((TOKENS, C), BF16),
            jax.ShapeDtypeStruct((TOKENS, KV), BF16),
        ],
        in_specs=[SMEM] + [VMEM] * 5 + [ANY] * 8,
        out_specs=[VMEM] * 3,
        scratch_shapes=[pltpu.VMEM((C, KV), BF16), pltpu.SemaphoreType.DMA((16,))],
        compiler_params=params(24),
        cost_estimate=pl.CostEstimate(flops=201_000_000, bytes_accessed=3_500_000, transcendentals=0),
    )(at, *parts, gain, *packed)


def query_kernel(at_ref, normed_ref, *refs):
    packed, (out_ref, w_ref, sems) = refs[:8], refs[8:]
    copies = []
    for array, slot, rel in PACKED:
        row = pl.multiple_of((at_ref[0] ^ rel) * 96, 96)
        copies.append((packed[array].at[slot, :, pl.ds(KV, QW)], w_ref.at[pl.ds(row, 96), :]))
    run_copies(copies, sems)
    queries = jnp.dot(normed_ref[...], w_ref[...], preferred_element_type=F32).astype(BF16)
    for head in range(HEADS):
        out_ref[head] = queries[:, head * HEAD_SIZE : (head + 1) * HEAD_SIZE]


def project_queries(at, normed, packed):
    return pl.pallas_call(
        query_kernel,
        out_shape=jax.ShapeDtypeStruct((HEADS, TOKENS, HEAD_SIZE), BF16),
        in_specs=[SMEM, VMEM] + [ANY] * 8,
        out_specs=VMEM,
        scratch_shapes=[pltpu.VMEM((C, QW), BF16), pltpu.SemaphoreType.DMA((16,))],
        compiler_params=params(24),
        cost_estimate=pl.CostEstimate(flops=805_000_000, bytes_accessed=4_500_000, transcendentals=0),
    )(at, normed, *packed)


def attend_kernel(n_blocks, first, scale_ref, q_ref, *refs):
    kvs, refs = refs[:n_blocks], refs[n_blocks:]
    if first:
        top_out, total_out, sum_out = refs
    else:
        top_ref, total_ref, sum_ref, top_out, total_out, sum_out = refs
    scale = scale_ref[pl.program_id(0)]
    q = q_ref[0]
    lanes = (TOKENS, HEAD_SIZE)
    scores, values = [], []
    for kv in kvs:
        keys = kv[:, :HEAD_SIZE]
        scores.append(
            lax.dot_general(q, keys, (((1,), (1,)), ((), ())), preferred_element_type=F32)
        )
        values.append(kv[:, HEAD_SIZE:])
    width = scores[0].shape[1]
    tall = scores[0]
    for s in scores[1:]:
        tall = jnp.maximum(tall, s)
    best = tall[:, :HEAD_SIZE]
    for i in range(1, width // HEAD_SIZE):
        best = jnp.maximum(best, tall[:, i * HEAD_SIZE : (i + 1) * HEAD_SIZE])
    top = jnp.broadcast_to(jnp.max(best, axis=1, keepdims=True), lanes)
    if not first:
        old = top_ref[0]
        top = jnp.maximum(top, old)
        fade = jnp.exp2((old - top) * scale)
    total = jnp.zeros(lanes, F32)
    summed = jnp.zeros(lanes, F32)
    for s, v in zip(scores, values):
        pieces = []
        for i in range(width // HEAD_SIZE):
            e = jnp.exp2((s[:, i * HEAD_SIZE : (i + 1) * HEAD_SIZE] - top) * scale)
            total = total + e
            pieces.append(e.astype(BF16))
        weights = jnp.concatenate(pieces, axis=1)
        summed = summed + jnp.dot(weights, v, preferred_element_type=F32)
    if not first:
        total = total + total_ref[0] * fade
        summed = summed + sum_ref[0] * fade
    top_out[0] = top
    total_out[0] = total
    sum_out[0] = summed


def attend(scale, queries, kvs, state):
    head = pl.BlockSpec((1, TOKENS, HEAD_SIZE), lambda h: (h, 0, 0))
    keys = sum(kv.shape[0] for kv in kvs)
    return pl.pallas_call(
        lambda *refs: attend_kernel(len(kvs), state is None, *refs),
        grid=(HEADS,),
        out_shape=[jax.ShapeDtypeStruct((HEADS, TOKENS, HEAD_SIZE), F32)] * 3,
        in_specs=[SMEM, head]
        + [pl.BlockSpec(kv.shape, lambda h: (0, 0)) for kv in kvs]
        + ([] if state is None else [head] * 3),
        out_specs=[head] * 3,
        compiler_params=params(32),
        cost_estimate=pl.CostEstimate(
            flops=4 * QW * TOKENS * keys,
            bytes_accessed=6_000_000,
            transcendentals=HEADS * TOKENS * keys,
        ),
    )(scale, queries, *kvs, *(state or ()))


def out_kernel(at_ref, total_ref, sum_ref, tokens_ref, *refs):
    packed, (out_ref, w_ref, sems) = refs[:8], refs[8:]
    copies = []
    for array, slot, rel in PACKED:
        row = pl.multiple_of((at_ref[0] ^ rel) * 64, 64)
        late = pl.multiple_of((at_ref[0] ^ rel) * 64 + 32, 32)
        source, start = packed[array], KV + QW
        copies.append((source.at[slot, pl.ds(0, 64), pl.ds(start, 1024)], w_ref.at[pl.ds(row, 64), pl.ds(0, 1024)]))
        copies.append((source.at[slot, pl.ds(64, 32), pl.ds(start, 512)], w_ref.at[pl.ds(row, 32), pl.ds(1024, 512)]))
        copies.append((source.at[slot, pl.ds(64, 32), pl.ds(start + 512, 512)], w_ref.at[pl.ds(late, 32), pl.ds(1024, 512)]))
    run_copies(copies, sems)
    heads = []
    for head in range(HEADS):
        total = jnp.sum(total_ref[head], axis=1, keepdims=True)
        heads.append((sum_ref[head] / total).astype(BF16))
    context = jnp.concatenate(heads, axis=1)
    update = jnp.dot(context, w_ref[...], preferred_element_type=F32)
    out_ref[...] = (update + tokens_ref[...].astype(F32)).astype(BF16)


def project_out(at, total, summed, tokens, packed):
    return pl.pallas_call(
        out_kernel,
        out_shape=jax.ShapeDtypeStruct((TOKENS, C), BF16),
        in_specs=[SMEM] + [VMEM] * 3 + [ANY] * 8,
        out_specs=VMEM,
        scratch_shapes=[pltpu.VMEM((QW, C), BF16), pltpu.SemaphoreType.DMA((48,))],
        compiler_params=params(32),
        cost_estimate=pl.CostEstimate(flops=805_000_000, bytes_accessed=7_000_000, transcendentals=0),
    )(at, total, summed, tokens, *packed)


def after(value, first):
    return lax.optimization_barrier((value, first))


def on_device(
    dna_features, conv_weight, conv_bias, norm_gain, query_weight, kv_weight, out_weight, head_scale
):
    dp, seq = lax.axis_index("dp"), lax.axis_index("seq")
    core, z = dp % 2, seq % 8
    quarter = z % 2 * 2 + core
    at = jnp.stack([dp, quarter]).astype(jnp.int32)

    shape = (KW, ROWS, QUARTER)
    keep = lax.dynamic_slice(conv_weight, (0, 0, quarter * QUARTER), shape)
    give = lax.dynamic_slice(conv_weight, (0, 0, (quarter ^ 1) * QUARTER), shape)
    got = receive(give, from_core)
    unit = jnp.concatenate(
        [jnp.where(core == 0, keep, got), jnp.where(core == 0, got, keep)], axis=1
    )
    x1, x3 = receive(unit, from_x(1)), receive(unit, from_x(3))
    y0 = receive(unit, from_y(1))
    x2 = receive(unit, from_x(2))
    y1, y3 = receive(x1, from_y(-1)), receive(x3, from_y(1))
    y2 = receive(x2, from_y(-1))
    units = (unit, x1, x3, x2, y0, y1, y3, y2)

    rows = dna_features.reshape(TOKENS, 2 * CIN)
    up = [(i, i + 1) for i in range(15)]
    before = lax.ppermute(rows[-1:], "seq", up)
    behind = lax.ppermute(rows[:1], "seq", [(j, i) for i, j in up])
    rows = jnp.concatenate([before, rows, behind], axis=0)
    rows_z = receive(rows, from_z_pair)
    rows_c = receive(rows, from_core)
    rows_d = receive(rows_z, from_core)
    blocks = jnp.stack(
        [
            jnp.concatenate([r[:TOKENS], r[1 : TOKENS + 1], r[2:]], axis=1)
            for r in (rows_d, rows_z, rows_c, rows)
        ]
    )
    bias = lax.dynamic_slice(conv_bias.reshape(1, C), (0, quarter * QUARTER), (1, QUARTER))

    tail = out_weight[:, QW:]
    packed_out = jnp.concatenate(
        [out_weight[:, :QW], jnp.concatenate([tail[:32], tail[32:]], axis=1)], axis=0
    )
    packed = jnp.concatenate([kv_weight, query_weight, packed_out], axis=1)
    packed, x2 = after(packed, x2)
    px1, px3, px2 = (receive(packed, from_x(s)) for s in (1, 3, 2))
    near = [jnp.stack([packed, px1]), jnp.stack([px3, px2])]
    near = near + [receive(near[0], from_y(1)), receive(near[1], from_y(-1))]
    packed = near + [receive(g, from_core) for g in near]

    t_d, t_z, t_c, t_own = convolve(at[:1] // 2, blocks, bias, units)
    parts = (t_own, receive(t_c, from_core), receive(t_z, from_z_pair), receive(t_d, from_diagonal))
    tokens, normed, pairs = norm_and_pairs(at, parts, norm_gain.reshape(1, C), packed)

    both = jnp.concatenate([pairs, receive(pairs, from_y_hi)], axis=0)
    below, above = receive(both, from_z(-1)), receive(both, from_z(1))
    groups = [[both], [below, above]]
    for _ in range(2):
        below, above = receive(below, from_z(-1)), receive(above, from_z(1))
        groups.append([below, above])
    groups.append([receive(below[:TOKENS], from_z(-1)), receive(above[TOKENS:], from_z(1))])

    queries = project_queries(at, normed, packed)
    scale = head_scale * (LOG2E / math.sqrt(HEAD_SIZE))
    state = None
    for group in groups:
        state = attend(scale, queries, group, state)
    encoded = project_out(at, state[1], state[2], tokens, packed)
    return tokens[None], encoded[None]


def solution(mesh):
    in_specs = (
        P("dp", "seq", None),
        P(None, "dp", None),
        P(),
        P(),
        P("dp", None),
        P("dp", None),
        P("dp", None),
        P(),
    )
    out_specs = (P("dp", "seq", None), P("dp", "seq", None))
    return jax.shard_map(
        on_device, mesh=mesh, in_specs=in_specs, out_specs=out_specs, check_vma=False
    )
```

time: 272 us -> 185 us (0.68)
  waiting for transfers between devices: 158 us -> 74.4 us
  matrix products: 48.4 us -> 0 us
  starting transfers between devices: 5.44 us -> 51.6 us
  Pallas kernels: 0 us -> 44.9 us
  blocking collectives: 23.9 us -> 0 us
  other arithmetic: 19.4 us -> 6.1 us
  between operations: 14 us -> 1.23 us
  local copies, waits for them, and re-layouts: 2.63 us -> 6.61 us
    all_gather x4 -> x0, waiting for transfers between devices: 156 us -> none  [the longest x1 86.3 us: on_device(): sequence_slice = lax.all_gather(pairs, 'seq', axis=1, tiled=True)]
    ppermute x2 -> x34, waiting for transfers between devices: 0.01 us -> 74.4 us  [the longest x32 74.4 us: receive(): return lax.ppermute(value, BOTH, pairs)]
    dot_general x10 -> x0, matrix products: 48.4 us -> none  [the longest x1 14.5 us: on_device(): jnp.einsum('eygl,ewl->egyw', query_matrix, sequence_slice[..., :HEAD_SIZE...]
    ppermute x2 -> x34, starting transfers between devices: 5.1 us -> 51.6 us  [the longest x32 45.7 us: receive(): return lax.ppermute(value, BOTH, pairs)]
    pallas_call x0 -> x9, Pallas kernels: none -> 44.9 us  [the longest x5 26.8 us: attend(): pl.pallas_call(lambda *refs: attend_kernel(len(kvs), state is None, *refs...]
    all_gather x1 -> x0, blocking collectives: 23.9 us -> none  [on_device(): pair_sum = project_rows(lax.all_gather(kv_weight, 'dp', axis=0, tiled=True))]
    reduce_sum x2 -> x0, other arithmetic: 14.8 us -> none  [the longest x1 14.6 us: on_device(): fresh_totals = totals_old * correction_scale + jnp.sum(weights, axis=-1)]
    reduce_max x1 -> x0, other arithmetic: 4.5 us -> none  [on_device(): jnp.max(activated.reshape(seq_rows, tok_rows, 2, C), axis=2)]
  transfers between devices with their start and end apart: 6 -> 34, of which waited for: 3 -> 13; matrix products, arithmetic and copies ran while one was open for 25% -> 6% of each run, Pallas kernels for 0% -> 18%
where the time goes in v1:
time: 185 us
  waiting for transfers between devices  74.4 us (40%)
  starting transfers between devices  51.6 us (28%)
  Pallas kernels  44.9 us (24%)
  local copies, waits for them, and re-layouts  6.61 us (4%)
  other arithmetic  6.1 us (3%)
    ppermute x32, waiting for transfers between devices, receive(): return lax.ppermute(value, BOTH, pairs)  74.4 us
    ppermute x32, starting transfers between devices, receive(): return lax.ppermute(value, BOTH, pairs)  45.7 us
    pallas_call x5, Pallas kernels, attend(): pl.pallas_call(lambda *refs: attend_kernel(len(kvs), state is None, *refs...  26.8 us
    pallas_call x1, Pallas kernels, convolve(): pl.pallas_call(conv_kernel, grid=(4,), out_shape=[jax.ShapeDtypeStruct((T...  9.97 us
    ppermute x1, starting transfers between devices, on_device(): before = lax.ppermute(rows[-1:], 'seq', up)  4.55 us
    pallas_call x1, Pallas kernels, project_out(): pl.pallas_call(out_kernel, out_shape=jax.ShapeDtypeStruct((TOKENS, C), BF...  3.86 us
  transfers between devices with their start and end apart: 34, of which 13 were waited for; matrix products, arithmetic and copies ran while one was open for 6% of the time, Pallas kernels for 18%

profile of v1, /device:TPU:2, one launch (start us, length us, event | category | flops | bytes accessed | tf_op | source)
XLA Modules:
  0.0 184.8 jit_solution(11623205754482173297)
XLA Ops:
  0.6 0.7 slice_bitcast_fusion.1
  1.4 1.3 collective-permute-start.1
  2.7 4.5 %collective-permute-start = (bf16[1,1536]{1,0:T(2,128)(2,1)S(1)}, bf16[1,1536]{1,0:T(2,128)(2,1)S(1)}, u32[]{:S(2)}, u32[]{:S(2)}) collective-permute-start(bf16[1,1536]{1,0:T(2,128)(2,1)S(1)} %bitcast.29), channel_id=1, source_target_pairs={{0,1},{1,2},{2,3},{3,4},{4,5},{5,6},{6,7},{7,8},{8,9},{9,10},{10,1... | collective-permute-start | bytes 9224 | tf_op jit(solution)/shard_map/ppermute | solution.py:324
  7.3 0.9 constant_dynamic-slice_fusion
  8.2 0.1 collective-permute-start.5
  8.3 0.8 fusion.6
  9.1 0.9 slice.80
  10.0 1.0 maximum_maximum_fusion
  11.0 1.4 reshape.18
  12.4 0.8 dynamic-slice.3
  13.2 0.2 pad_maximum_fusion.5
  13.4 0.6 collective-permute-start.4
  14.0 1.9 %collective-permute-start.2 = (bf16[258,1536]{1,0:T(8,128)(2,1)S(1)}, bf16[258,1536]{1,0:T(8,128)(2,1)S(1)}, u32[]{:S(2)}, u32[]{:S(2)}) collective-permute-start(bf16[258,1536]{1,0:T(8,128)(2,1)S(1)} %pad_maximum_fusion.5), channel_id=1, source_target_pairs={{1,0},{0,1},{3,2},{2,3},{5,4},{4,5},{7,6},{6,7},{9,8},{8,9},{11,10... | collective-permute-start | bytes 2377736 | tf_op jit(solution)/shard_map/ppermute | solution.py:39
  15.9 1.0 broadcast_select_fusion.1
  16.9 2.2 %collective-permute-start.8 = (bf16[5,96,384]{2,1,0:T(8,128)(2,1)S(1)}, bf16[5,96,384]{2,1,0:T(8,128)(2,1)S(1)}, u32[]{:S(2)}, u32[]{:S(2)}) collective-permute-start(bf16[5,96,384]{2,1,0:T(8,128)(2,1)S(1)} %pad_maximum_fusion.6.refs_0_), channel_id=1, source_target_pairs={{128,0},{129,1},{130,2},{131,3},{132,4},{133,5},{134,6},{135,7},{1... | collective-permute-start | bytes 1105928 | tf_op jit(solution)/shard_map/ppermute | solution.py:39
  19.1 1.9 %fusion.1 = bf16[1,256,4608]{2,1,0:T(8,128)(2,1)S(1)} fusion(bf16[1,1536]{1,0:T(2,128)(2,1)S(1)} %collective-permute-done.1, bf16[256,1536]{1,0:T(8,128)(2,1)S(1)} %reshape.18, bf16[1,1536]{1,0:T(2,128)(2,1)S(1)} %collective-permute-done), kind=kLoop, calls=%fused_computation.3 | loop fusion | flops 11796480 | bytes 3151872 | tf_op jit(solution)/shard_map/stack | solution.py:330
  21.1 1.5 collective-permute-start.6
  22.6 0.5 collective-permute-start.7
  23.1 6.9 %collective-permute-done.8.refs_3_ = bf16[5,96,384]{2,1,0:T(8,128)(2,1)S(1)} collective-permute-done((bf16[5,96,384]{2,1,0:T(8,128)(2,1)S(1)}, bf16[5,96,384]{2,1,0:T(8,128)(2,1)S(1)}, u32[]{:S(2)}, u32[]{:S(2)}) %collective-permute-start.8) | collective-permute-done | bytes 368672 | tf_op jit(solution)/shard_map/ppermute | solution.py:39
  30.0 0.5 collective-permute-start.16
  30.6 2.4 %collective-permute-start.18 = (bf16[96,2304]{1,0:T(8,128)(2,1)S(1)}, bf16[96,2304]{1,0:T(8,128)(2,1)S(1)}, u32[]{:S(2)}, u32[]{:S(2)}) collective-permute-start(bf16[96,2304]{1,0:T(8,128)(2,1)S(1)} %maximum_maximum_fusion), channel_id=1, source_target_pairs={{128,0},{129,1},{130,2},{131,3},{132,4},{133,5},{134,6},{135,7},{1... | collective-permute-start | bytes 1327112 | tf_op jit(solution)/shard_map/ppermute | solution.py:39
  33.0 0.3 fusion.5
  33.3 0.2 maximum_bitcast_fusion.2
  33.5 0.7 collective-permute-done.2
  34.2 1.5 collective-permute-start.17
  35.7 11.7 %collective-permute-done.16 = bf16[96,2304]{1,0:T(8,128)(2,1)S(1)} collective-permute-done((bf16[96,2304]{1,0:T(8,128)(2,1)S(1)}, bf16[96,2304]{1,0:T(8,128)(2,1)S(1)}, u32[]{:S(2)}, u32[]{:S(2)}) %collective-permute-start.16) | collective-permute-done | bytes 442400 | tf_op jit(solution)/shard_map/ppermute | solution.py:39
  47.5 0.3 fusion.4
  47.9 6.5 %collective-permute-start.9 = (bf16[5,96,384]{2,1,0:T(8,128)(2,1)S(1)}, bf16[5,96,384]{2,1,0:T(8,128)(2,1)S(1)}, u32[]{:S(2)}, u32[]{:S(2)}) collective-permute-start(bf16[5,96,384]{2,1,0:T(8,128)(2,1)S(1)} %pad_maximum_fusion.6.refs_0_), channel_id=1, source_target_pairs={{32,0},{33,1},{34,2},{35,3},{36,4},{37,5},{38,6},{39,7},{40,8},{41... | collective-permute-start | bytes 1105928 | tf_op jit(solution)/shard_map/ppermute | solution.py:39
  54.4 1.3 collective-permute-done.18
  55.7 1.6 collective-permute-start.10
  57.3 6.7 %collective-permute-start.11 = (bf16[5,96,384]{2,1,0:T(8,128)(2,1)S(1)}, bf16[5,96,384]{2,1,0:T(8,128)(2,1)S(1)}, u32[]{:S(2)}, u32[]{:S(2)}) collective-permute-start(bf16[5,96,384]{2,1,0:T(8,128)(2,1)S(1)} %collective-permute-done.7.refs_2_), channel_id=1, source_target_pairs={{32,0},{33,1},{34,2},{35,3},{36,4},{37,5},{38,6},{39,7},{40,8},{41... | collective-permute-start | bytes 1105928 | tf_op jit(solution)/shard_map/ppermute | solution.py:39
  64.1 1.2 collective-permute-start.19
  65.3 0.3 fusion.3
  65.7 0.4 maximum_bitcast_fusion
  66.0 1.1 collective-permute-start.20
  67.1 1.2 pad_maximum_fusion.a_ref
  68.4 6.6 %collective-permute-done.10.refs_5_ = bf16[5,96,384]{2,1,0:T(8,128)(2,1)S(1)} collective-permute-done((bf16[5,96,384]{2,1,0:T(8,128)(2,1)S(1)}, bf16[5,96,384]{2,1,0:T(8,128)(2,1)S(1)}, u32[]{:S(2)}, u32[]{:S(2)}) %collective-permute-start.10) | collective-permute-done | bytes 368672 | tf_op jit(solution)/shard_map/ppermute | solution.py:39
  75.0 0.5 collective-permute-start.22
  75.5 14.3 %collective-permute-done.19.refs_7_.refs_2_ = bf16[2,96,2304]{2,1,0:T(8,128)(2,1)S(1)} collective-permute-done((bf16[2,96,2304]{2,1,0:T(8,128)(2,1)S(1)}, bf16[2,96,2304]{2,1,0:T(8,128)(2,1)S(1)}, u32[]{:S(2)}, u32[]{:S(2)}) %collective-permute-start.19) | collective-permute-done | bytes 884768 | tf_op jit(solution)/shard_map/ppermute | solution.py:39
  89.8 3.4 %collective-permute-done.20.refs_8_.refs_3_ = bf16[2,96,2304]{2,1,0:T(8,128)(2,1)S(1)} collective-permute-done((bf16[2,96,2304]{2,1,0:T(8,128)(2,1)S(1)}, bf16[2,96,2304]{2,1,0:T(8,128)(2,1)S(1)}, u32[]{:S(2)}, u32[]{:S(2)}) %collective-permute-start.20) | collective-permute-done | bytes 884768 | tf_op jit(solution)/shard_map/ppermute | solution.py:39
  93.2 10.0 %shard_map.95 = (bf16[256,384]{1,0:T(8,128)(2,1)S(1)}, bf16[256,384]{1,0:T(8,128)(2,1)S(1)}, bf16[256,384]{1,0:T(8,128)(2,1)S(1)}, bf16[256,384]{1,0:T(8,128)(2,1)S(1)}) custom-call(s32[1]{0:T(128)S(6)} %select_n.42.at_ref, bf16[4,256,4608]{2,1,0:T(8,128)(2,1)S(1)} %pad_maximum_fusion.a_ref, f32[1,384]{1,0:T(1,128)S(1)} %dynamic_slice.9.bias_ref, ...), custom_call_target="tpu_custom_call" | custom-call | flops 6040000000 | bytes 14000000 | tf_op jit(solution)/shard_map/pallas_call | solution.py:119
  103.2 0.6 collective-permute-start.13
  103.8 1.1 collective-permute-done.13.refs_1_
  104.9 2.0 %collective-permute-start.14 = (bf16[256,384]{1,0:T(8,128)(2,1)S(1)}, bf16[256,384]{1,0:T(8,128)(2,1)S(1)}, u32[]{:S(2)}, u32[]{:S(2)}) collective-permute-start(bf16[256,384]{1,0:T(8,128)(2,1)S(1)} %get-tuple-element.26), channel_id=1, source_target_pairs={{1,0},{0,1},{3,2},{2,3},{5,4},{4,5},{7,6},{6,7},{9,8},{8,9},{11,10... | collective-permute-start | bytes 589832 | tf_op jit(solution)/shard_map/ppermute | solution.py:39
  106.9 5.4 %collective-permute-done.14.refs_2_ = bf16[256,384]{1,0:T(8,128)(2,1)S(1)} collective-permute-done((bf16[256,384]{1,0:T(8,128)(2,1)S(1)}, bf16[256,384]{1,0:T(8,128)(2,1)S(1)}, u32[]{:S(2)}, u32[]{:S(2)}) %collective-permute-start.14) | collective-permute-done | bytes 196640 | tf_op jit(solution)/shard_map/ppermute | solution.py:39
  112.3 0.9 collective-permute-start.15
  113.3 5.9 %collective-permute-done.15.refs_3_ = bf16[256,384]{1,0:T(8,128)(2,1)S(1)} collective-permute-done((bf16[256,384]{1,0:T(8,128)(2,1)S(1)}, bf16[256,384]{1,0:T(8,128)(2,1)S(1)}, u32[]{:S(2)}, u32[]{:S(2)}) %collective-permute-start.15) | collective-permute-done | bytes 196640 | tf_op jit(solution)/shard_map/ppermute | solution.py:39
  119.3 2.1 %shard_map.96 = (bf16[256,1536]{1,0:T(8,128)(2,1)}, bf16[256,1536]{1,0:T(8,128)(2,1)S(1)}, bf16[256,256]{1,0:T(8,128)(2,1)S(1)}) custom-call(s32[2]{0:T(128)S(1)} %pad_add_fusion.at_ref, bf16[256,384]{1,0:T(8,128)(2,1)S(1)} %get-tuple-element.24.refs_0_, bf16[256,384]{1,0:T(8,128)(2,1)S(1)} %collective-permute-done.13.refs_1_, ...), custom_call_target="tpu_custom_call" | custom-call | flops 201000000 | bytes 3500000 | tf_op jit(solution)/shard_map/pallas_call | solution.py:159
  121.4 0.1 collective-permute-start.25
  121.5 7.0 %collective-permute-done.25 = bf16[256,256]{1,0:T(8,128)(2,1)S(1)} collective-permute-done((bf16[256,256]{1,0:T(8,128)(2,1)S(1)}, bf16[256,256]{1,0:T(8,128)(2,1)S(1)}, u32[]{:S(2)}, u32[]{:S(2)}) %collective-permute-start.25) | collective-permute-done | bytes 131104 | tf_op jit(solution)/shard_map/ppermute | solution.py:39
  128.5 1.6 collective-permute-start.26
  130.1 1.7 collective-permute-start.30
  131.8 5.5 %collective-permute-done.26.refs_2_ = bf16[512,256]{1,0:T(8,128)(2,1)S(1)} collective-permute-done((bf16[512,256]{1,0:T(8,128)(2,1)S(1)}, bf16[512,256]{1,0:T(8,128)(2,1)S(1)}, u32[]{:S(2)}, u32[]{:S(2)}) %collective-permute-start.26) | collective-permute-done | bytes 262176 | tf_op jit(solution)/shard_map/ppermute | solution.py:39
  137.3 3.2 %collective-permute-start.31 = (bf16[512,256]{1,0:T(8,128)(2,1)S(1)}, bf16[512,256]{1,0:T(8,128)(2,1)S(1)}, u32[]{:S(2)}, u32[]{:S(2)}) collective-permute-start(bf16[512,256]{1,0:T(8,128)(2,1)S(1)} %collective-permute-done.30.refs_3_), channel_id=1, source_target_pairs={{1,0},{2,1},{3,2},{4,3},{5,4},{6,5},{7,6},{0,7},{9,8},{10,9},{11,1... | collective-permute-start | bytes 786440 | tf_op jit(solution)/shard_map/ppermute | solution.py:39
  140.5 4.5 %collective-permute-done.27.refs_2_ = bf16[512,256]{1,0:T(8,128)(2,1)S(1)} collective-permute-done((bf16[512,256]{1,0:T(8,128)(2,1)S(1)}, bf16[512,256]{1,0:T(8,128)(2,1)S(1)}, u32[]{:S(2)}, u32[]{:S(2)}) %collective-permute-start.27) | collective-permute-done | bytes 262176 | tf_op jit(solution)/shard_map/ppermute | solution.py:39
  145.1 3.2 %collective-permute-start.32 = (bf16[512,256]{1,0:T(8,128)(2,1)S(1)}, bf16[512,256]{1,0:T(8,128)(2,1)S(1)}, u32[]{:S(2)}, u32[]{:S(2)}) collective-permute-start(bf16[512,256]{1,0:T(8,128)(2,1)S(1)} %collective-permute-done.31.refs_3_), channel_id=1, source_target_pairs={{1,0},{2,1},{3,2},{4,3},{5,4},{6,5},{7,6},{0,7},{9,8},{10,9},{11,1... | collective-permute-start | bytes 786440 | tf_op jit(solution)/shard_map/ppermute | solution.py:39
  148.3 2.1 %shard_map.97.refs_1_ = bf16[8,256,128]{2,1,0:T(8,128)(2,1)S(1)} custom-call(s32[2]{0:T(128)S(1)} %pad_add_fusion.at_ref, bf16[256,1536]{1,0:T(8,128)(2,1)S(1)} %get-tuple-element.30.normed_ref, bf16[2,96,2304]{2,1,0:T(8,128)(2,1)S(1)} %pad_maximum_fusion.3.refs_5_.refs_0_, bf16[2,96,2304]{2,1,0:T(8,128)(2,1)S(1)} %pad_maximum_fusion.4.refs_6_.refs_1_, ...), custom_call_target="tpu_custom_call" | custom-call | flops 805000000 | bytes 4500000 | tf_op jit(solution)/shard_map/pallas_call | solution.py:187
  150.4 4.3 %shard_map.98 = (f32[8,256,128]{2,1,0:T(8,128)S(1)}, f32[8,256,128]{2,1,0:T(8,128)S(1)}, f32[8,256,128]{2,1,0:T(8,128)S(1)}) custom-call(f32[8]{0:T(128)S(1)} %broadcast_multiply_fusion.refs_0_, bf16[8,256,128]{2,1,0:T(8,128)(2,1)S(1)} %shard_map.97.refs_1_, bf16[512,256]{1,0:T(8,128)(2,1)S(1)} %constant_dynamic-update-slice_fusion.refs_2_), custom_call_target="tpu_custom_call" | custom-call | flops 536870912 | bytes 6000000 | tf_op jit(solution)/shard_map/pallas_call | solution.py:247
  154.8 5.8 %shard_map.99 = (f32[8,256,128]{2,1,0:T(8,128)S(1)}, f32[8,256,128]{2,1,0:T(8,128)S(1)}, f32[8,256,128]{2,1,0:T(8,128)S(1)}) custom-call(f32[8]{0:T(128)S(1)} %broadcast_multiply_fusion.refs_0_, bf16[8,256,128]{2,1,0:T(8,128)(2,1)S(1)} %shard_map.97.refs_1_, bf16[512,256]{1,0:T(8,128)(2,1)S(1)} %collective-permute-done.26.refs_2_, ...), custom_call_target="tpu_custom_call" | custom-call | flops 1073741824 | bytes 6000000 | tf_op jit(solution)/shard_map/pallas_call | solution.py:247
  160.7 3.3 %collective-permute-start.33 = (bf16[256,256]{1,0:T(8,128)(2,1)S(1)}, bf16[256,256]{1,0:T(8,128)(2,1)S(1)}, u32[]{:S(2)}, u32[]{:S(2)}) collective-permute-start(bf16[256,256]{1,0:T(8,128)(2,1)S(1)} %slice.95), channel_id=1, source_target_pairs={{1,0},{2,1},{3,2},{4,3},{5,4},{6,5},{7,6},{0,7},{9,8},{10,9},{11,1... | collective-permute-start | bytes 393224 | tf_op jit(solution)/shard_map/ppermute | solution.py:39
  164.0 5.8 %shard_map.100 = (f32[8,256,128]{2,1,0:T(8,128)S(1)}, f32[8,256,128]{2,1,0:T(8,128)S(1)}, f32[8,256,128]{2,1,0:T(8,128)S(1)}) custom-call(f32[8]{0:T(128)S(1)} %broadcast_multiply_fusion.refs_0_, bf16[8,256,128]{2,1,0:T(8,128)(2,1)S(1)} %shard_map.97.refs_1_, bf16[512,256]{1,0:T(8,128)(2,1)S(1)} %collective-permute-done.27.refs_2_, ...), custom_call_target="tpu_custom_call" | custom-call | flops 1073741824 | bytes 6000000 | tf_op jit(solution)/shard_map/pallas_call | solution.py:247
  169.8 5.8 %shard_map.101 = (f32[8,256,128]{2,1,0:T(8,128)S(1)}, f32[8,256,128]{2,1,0:T(8,128)S(1)}, f32[8,256,128]{2,1,0:T(8,128)S(1)}) custom-call(f32[8]{0:T(128)S(1)} %broadcast_multiply_fusion.refs_0_, bf16[8,256,128]{2,1,0:T(8,128)(2,1)S(1)} %shard_map.97.refs_1_, bf16[512,256]{1,0:T(8,128)(2,1)S(1)} %collective-permute-done.28.refs_2_, ...), custom_call_target="tpu_custom_call" | custom-call | flops 1073741824 | bytes 6000000 | tf_op jit(solution)/shard_map/pallas_call | solution.py:247
  175.6 5.1 %shard_map.102 = (f32[8,256,128]{2,1,0:T(8,128)}, f32[8,256,128]{2,1,0:T(8,128)S(1)}, f32[8,256,128]{2,1,0:T(8,128)S(1)}) custom-call(f32[8]{0:T(128)S(1)} %broadcast_multiply_fusion.refs_0_, bf16[8,256,128]{2,1,0:T(8,128)(2,1)S(1)} %shard_map.97.refs_1_, bf16[256,256]{1,0:T(8,128)(2,1)S(1)} %collective-permute-done.29.refs_2_, ...), custom_call_target="tpu_custom_call" | custom-call | flops 536870912 | bytes 6000000 | tf_op jit(solution)/shard_map/pallas_call | solution.py:247
  180.7 3.9 %shard_map.103 = bf16[256,1536]{1,0:T(8,128)(2,1)} custom-call(s32[2]{0:T(128)S(1)} %pad_add_fusion.at_ref, f32[8,256,128]{2,1,0:T(8,128)S(1)} %get-tuple-element.44.total_ref, f32[8,256,128]{2,1,0:T(8,128)S(1)} %get-tuple-element.45.sum_ref, bf16[256,1536]{1,0:T(8,128)(2,1)S(1)} %copy-done, bf16[2,96,2304]{2,1,0:T(8,128)(2,1)S(1)} %pad_maximum_fusion.3.refs_5_.refs_0_, ...), custom_call_target="tpu_custom_call" | custom-call | flops 805000000 | bytes 7000000 | tf_op jit(solution)/shard_map/pallas_call | solution.py:285
  (48 shorter events, 0.5 us)
Async XLA Ops:
  1.4 11.8 %collective-permute-start.1 = (bf16[1,1536]{1,0:T(2,128)(2,1)S(1)}, bf16[1,1536]{1,0:T(2,128)(2,1)S(1)}, u32[]{:S(2)}, u32[]{:S(2)}) collective-permute-start(bf16[1,1536]{1,0:T(2,128)(2,1)S(1)} %bitcast.28), channel_id=1, source_target_pairs={{1,0},{2,1},{3,2},{4,3},{5,4},{6,5},{7,6},{8,7},{9,8},{10,9},{11,1... | collective-permute-start | bytes 9224 | tf_op jit(solution)/shard_map/ppermute | solution.py:325
  2.7 10.5 %collective-permute-start = (bf16[1,1536]{1,0:T(2,128)(2,1)S(1)}, bf16[1,1536]{1,0:T(2,128)(2,1)S(1)}, u32[]{:S(2)}, u32[]{:S(2)}) collective-permute-start(bf16[1,1536]{1,0:T(2,128)(2,1)S(1)} %bitcast.29), channel_id=1, source_target_pairs={{0,1},{1,2},{2,3},{3,4},{4,5},{5,6},{6,7},{7,8},{8,9},{9,10},{10,1... | collective-permute-start | bytes 9224 | tf_op jit(solution)/shard_map/ppermute | solution.py:324
  8.2 7.6 %collective-permute-start.5 = (bf16[5,48,384]{2,1,0:T(8,128)(2,1)S(1)}, bf16[5,48,384]{2,1,0:T(8,128)(2,1)S(1)}, u32[]{:S(2)}, u32[]{:S(2)}) collective-permute-start(bf16[5,48,384]{2,1,0:T(8,128)(2,1)S(1)} %constant_dynamic-slice_fusion), channel_id=1, source_target_pairs={{16,0},{17,1},{18,2},{19,3},{20,4},{21,5},{22,6},{23,7},{24,8},{25... | collective-permute-start | bytes 552968 | tf_op jit(solution)/shard_map/ppermute | solution.py:39
  13.4 17.2 %collective-permute-start.4 = (bf16[258,1536]{1,0:T(8,128)(2,1)S(1)}, bf16[258,1536]{1,0:T(8,128)(2,1)S(1)}, u32[]{:S(2)}, u32[]{:S(2)}) collective-permute-start(bf16[258,1536]{1,0:T(8,128)(2,1)S(1)} %pad_maximum_fusion.5), channel_id=1, source_target_pairs={{16,0},{17,1},{18,2},{19,3},{20,4},{21,5},{22,6},{23,7},{24,8},{25... | collective-permute-start | bytes 2377736 | tf_op jit(solution)/shard_map/ppermute | solution.py:39
  14.0 20.2 %collective-permute-start.2 = (bf16[258,1536]{1,0:T(8,128)(2,1)S(1)}, bf16[258,1536]{1,0:T(8,128)(2,1)S(1)}, u32[]{:S(2)}, u32[]{:S(2)}) collective-permute-start(bf16[258,1536]{1,0:T(8,128)(2,1)S(1)} %pad_maximum_fusion.5), channel_id=1, source_target_pairs={{1,0},{0,1},{3,2},{2,3},{5,4},{4,5},{7,6},{6,7},{9,8},{8,9},{11,10... | collective-permute-start | bytes 2377736 | tf_op jit(solution)/shard_map/ppermute | solution.py:39
  16.9 13.1 %collective-permute-start.8 = (bf16[5,96,384]{2,1,0:T(8,128)(2,1)S(1)}, bf16[5,96,384]{2,1,0:T(8,128)(2,1)S(1)}, u32[]{:S(2)}, u32[]{:S(2)}) collective-permute-start(bf16[5,96,384]{2,1,0:T(8,128)(2,1)S(1)} %pad_maximum_fusion.6.refs_0_), channel_id=1, source_target_pairs={{128,0},{129,1},{130,2},{131,3},{132,4},{133,5},{134,6},{135,7},{1... | collective-permute-start | bytes 1105928 | tf_op jit(solution)/shard_map/ppermute | solution.py:39
  21.1 26.8 %collective-permute-start.6 = (bf16[5,96,384]{2,1,0:T(8,128)(2,1)S(1)}, bf16[5,96,384]{2,1,0:T(8,128)(2,1)S(1)}, u32[]{:S(2)}, u32[]{:S(2)}) collective-permute-start(bf16[5,96,384]{2,1,0:T(8,128)(2,1)S(1)} %pad_maximum_fusion.6.refs_0_), channel_id=1, source_target_pairs={{64,0},{65,1},{66,2},{67,3},{68,4},{69,5},{70,6},{71,7},{72,8},{73... | collective-permute-start | bytes 1105928 | tf_op jit(solution)/shard_map/ppermute | solution.py:39
  22.6 31.8 %collective-permute-start.7 = (bf16[5,96,384]{2,1,0:T(8,128)(2,1)S(1)}, bf16[5,96,384]{2,1,0:T(8,128)(2,1)S(1)}, u32[]{:S(2)}, u32[]{:S(2)}) collective-permute-start(bf16[5,96,384]{2,1,0:T(8,128)(2,1)S(1)} %pad_maximum_fusion.6.refs_0_), channel_id=1, source_target_pairs={{192,0},{193,1},{194,2},{195,3},{196,4},{197,5},{198,6},{199,7},{2... | collective-permute-start | bytes 1105928 | tf_op jit(solution)/shard_map/ppermute | solution.py:39
  30.0 17.4 %collective-permute-start.16 = (bf16[96,2304]{1,0:T(8,128)(2,1)S(1)}, bf16[96,2304]{1,0:T(8,128)(2,1)S(1)}, u32[]{:S(2)}, u32[]{:S(2)}) collective-permute-start(bf16[96,2304]{1,0:T(8,128)(2,1)S(1)} %maximum_maximum_fusion), channel_id=1, source_target_pairs={{64,0},{65,1},{66,2},{67,3},{68,4},{69,5},{70,6},{71,7},{72,8},{73... | collective-permute-start | bytes 1327112 | tf_op jit(solution)/shard_map/ppermute | solution.py:39
  30.6 25.2 %collective-permute-start.18 = (bf16[96,2304]{1,0:T(8,128)(2,1)S(1)}, bf16[96,2304]{1,0:T(8,128)(2,1)S(1)}, u32[]{:S(2)}, u32[]{:S(2)}) collective-permute-start(bf16[96,2304]{1,0:T(8,128)(2,1)S(1)} %maximum_maximum_fusion), channel_id=1, source_target_pairs={{128,0},{129,1},{130,2},{131,3},{132,4},{133,5},{134,6},{135,7},{1... | collective-permute-start | bytes 1327112 | tf_op jit(solution)/shard_map/ppermute | solution.py:39
  34.2 23.1 %collective-permute-start.17 = (bf16[96,2304]{1,0:T(8,128)(2,1)S(1)}, bf16[96,2304]{1,0:T(8,128)(2,1)S(1)}, u32[]{:S(2)}, u32[]{:S(2)}) collective-permute-start(bf16[96,2304]{1,0:T(8,128)(2,1)S(1)} %maximum_maximum_fusion), channel_id=1, source_target_pairs={{192,0},{193,1},{194,2},{195,3},{196,4},{197,5},{198,6},{199,7},{2... | collective-permute-start | bytes 1327112 | tf_op jit(solution)/shard_map/ppermute | solution.py:39
  47.4 16.6 %collective-permute-start.3 = (bf16[258,1536]{1,0:T(8,128)(2,1)S(1)}, bf16[258,1536]{1,0:T(8,128)(2,1)S(1)}, u32[]{:S(2)}, u32[]{:S(2)}) collective-permute-start(bf16[258,1536]{1,0:T(8,128)(2,1)S(1)} %collective-permute-done.2), channel_id=1, source_target_pairs={{16,0},{17,1},{18,2},{19,3},{20,4},{21,5},{22,6},{23,7},{24,8},{25... | collective-permute-start | bytes 2377736 | tf_op jit(solution)/shard_map/ppermute | solution.py:39
  47.9 18.1 %collective-permute-start.9 = (bf16[5,96,384]{2,1,0:T(8,128)(2,1)S(1)}, bf16[5,96,384]{2,1,0:T(8,128)(2,1)S(1)}, u32[]{:S(2)}, u32[]{:S(2)}) collective-permute-start(bf16[5,96,384]{2,1,0:T(8,128)(2,1)S(1)} %pad_maximum_fusion.6.refs_0_), channel_id=1, source_target_pairs={{32,0},{33,1},{34,2},{35,3},{36,4},{37,5},{38,6},{39,7},{40,8},{41... | collective-permute-start | bytes 1105928 | tf_op jit(solution)/shard_map/ppermute | solution.py:39
  54.4 38.8 %collective-permute-start.12 = (bf16[5,96,384]{2,1,0:T(8,128)(2,1)S(1)}, bf16[5,96,384]{2,1,0:T(8,128)(2,1)S(1)}, u32[]{:S(2)}, u32[]{:S(2)}) collective-permute-start(bf16[5,96,384]{2,1,0:T(8,128)(2,1)S(1)} %collective-permute-done.8.refs_3_), channel_id=1, source_target_pairs={{40,0},{41,1},{42,2},{43,3},{44,4},{45,5},{46,6},{47,7},{32,8},{33... | collective-permute-start | bytes 1105928 | tf_op jit(solution)/shard_map/ppermute | solution.py:39
  55.7 19.2 %collective-permute-start.10 = (bf16[5,96,384]{2,1,0:T(8,128)(2,1)S(1)}, bf16[5,96,384]{2,1,0:T(8,128)(2,1)S(1)}, u32[]{:S(2)}, u32[]{:S(2)}) collective-permute-start(bf16[5,96,384]{2,1,0:T(8,128)(2,1)S(1)} %collective-permute-done.6.refs_1_), channel_id=1, source_target_pairs={{40,0},{41,1},{42,2},{43,3},{44,4},{45,5},{46,6},{47,7},{32,8},{33... | collective-permute-start | bytes 1105928 | tf_op jit(solution)/shard_map/ppermute | solution.py:39
  57.3 17.7 %collective-permute-start.11 = (bf16[5,96,384]{2,1,0:T(8,128)(2,1)S(1)}, bf16[5,96,384]{2,1,0:T(8,128)(2,1)S(1)}, u32[]{:S(2)}, u32[]{:S(2)}) collective-permute-start(bf16[5,96,384]{2,1,0:T(8,128)(2,1)S(1)} %collective-permute-done.7.refs_2_), channel_id=1, source_target_pairs={{32,0},{33,1},{34,2},{35,3},{36,4},{37,5},{38,6},{39,7},{40,8},{41... | collective-permute-start | bytes 1105928 | tf_op jit(solution)/shard_map/ppermute | solution.py:39
  64.1 25.7 %collective-permute-start.19 = (bf16[2,96,2304]{2,1,0:T(8,128)(2,1)S(1)}, bf16[2,96,2304]{2,1,0:T(8,128)(2,1)S(1)}, u32[]{:S(2)}, u32[]{:S(2)}) collective-permute-start(bf16[2,96,2304]{2,1,0:T(8,128)(2,1)S(1)} %pad_maximum_fusion.3.refs_5_.refs_0_), channel_id=1, source_target_pairs={{32,0},{33,1},{34,2},{35,3},{36,4},{37,5},{38,6},{39,7},{40,8},{41... | collective-permute-start | bytes 2654216 | tf_op jit(solution)/shard_map/ppermute | solution.py:39
  66.0 27.2 %collective-permute-start.20 = (bf16[2,96,2304]{2,1,0:T(8,128)(2,1)S(1)}, bf16[2,96,2304]{2,1,0:T(8,128)(2,1)S(1)}, u32[]{:S(2)}, u32[]{:S(2)}) collective-permute-start(bf16[2,96,2304]{2,1,0:T(8,128)(2,1)S(1)} %pad_maximum_fusion.4.refs_6_.refs_1_), channel_id=1, source_target_pairs={{40,0},{41,1},{42,2},{43,3},{44,4},{45,5},{46,6},{47,7},{32,8},{33... | collective-permute-start | bytes 2654216 | tf_op jit(solution)/shard_map/ppermute | solution.py:39
  68.4 44.9 %copy-start.1 = (f32[1536]{0:T(1024)S(1)}, f32[1536]{0:T(1024)}, u32[]{:S(2)}) copy-start(f32[1536]{0:T(1024)} %param.11) | copy-start | bytes 18436
  75.0 44.3 %collective-permute-start.21 = (bf16[2,96,2304]{2,1,0:T(8,128)(2,1)S(1)}, bf16[2,96,2304]{2,1,0:T(8,128)(2,1)S(1)}, u32[]{:S(2)}, u32[]{:S(2)}) collective-permute-start(bf16[2,96,2304]{2,1,0:T(8,128)(2,1)S(1)} %pad_maximum_fusion.3.refs_5_.refs_0_), channel_id=1, source_target_pairs={{16,0},{17,1},{18,2},{19,3},{20,4},{21,5},{22,6},{23,7},{24,8},{25... | collective-permute-start | bytes 2654216 | tf_op jit(solution)/shard_map/ppermute | solution.py:39
  75.0 44.3 %collective-permute-start.22 = (bf16[2,96,2304]{2,1,0:T(8,128)(2,1)S(1)}, bf16[2,96,2304]{2,1,0:T(8,128)(2,1)S(1)}, u32[]{:S(2)}, u32[]{:S(2)}) collective-permute-start(bf16[2,96,2304]{2,1,0:T(8,128)(2,1)S(1)} %pad_maximum_fusion.4.refs_6_.refs_1_), channel_id=1, source_target_pairs={{16,0},{17,1},{18,2},{19,3},{20,4},{21,5},{22,6},{23,7},{24,8},{25... | collective-permute-start | bytes 2654216 | tf_op jit(solution)/shard_map/ppermute | solution.py:39
  89.8 29.4 %collective-permute-start.23 = (bf16[2,96,2304]{2,1,0:T(8,128)(2,1)S(1)}, bf16[2,96,2304]{2,1,0:T(8,128)(2,1)S(1)}, u32[]{:S(2)}, u32[]{:S(2)}) collective-permute-start(bf16[2,96,2304]{2,1,0:T(8,128)(2,1)S(1)} %collective-permute-done.19.refs_7_.refs_2_), channel_id=1, source_target_pairs={{16,0},{17,1},{18,2},{19,3},{20,4},{21,5},{22,6},{23,7},{24,8},{25... | collective-permute-start | bytes 2654216 | tf_op jit(solution)/shard_map/ppermute | solution.py:39
  93.2 26.0 %collective-permute-start.24 = (bf16[2,96,2304]{2,1,0:T(8,128)(2,1)S(1)}, bf16[2,96,2304]{2,1,0:T(8,128)(2,1)S(1)}, u32[]{:S(2)}, u32[]{:S(2)}) collective-permute-start(bf16[2,96,2304]{2,1,0:T(8,128)(2,1)S(1)} %collective-permute-done.20.refs_8_.refs_3_), channel_id=1, source_target_pairs={{16,0},{17,1},{18,2},{19,3},{20,4},{21,5},{22,6},{23,7},{24,8},{25... | collective-permute-start | bytes 2654216 | tf_op jit(solution)/shard_map/ppermute | solution.py:39
  103.2 45.1 %copy-start.2 = (f32[8]{0:T(128)S(1)}, f32[8]{0:T(128)}, u32[]{:S(2)}) copy-start(f32[8]{0:T(128)} %param.15) | copy-start | bytes 100
  103.2 1.7 collective-permute-start.13
  104.9 7.4 %collective-permute-start.14 = (bf16[256,384]{1,0:T(8,128)(2,1)S(1)}, bf16[256,384]{1,0:T(8,128)(2,1)S(1)}, u32[]{:S(2)}, u32[]{:S(2)}) collective-permute-start(bf16[256,384]{1,0:T(8,128)(2,1)S(1)} %get-tuple-element.26), channel_id=1, source_target_pairs={{1,0},{0,1},{3,2},{2,3},{5,4},{4,5},{7,6},{6,7},{9,8},{8,9},{11,10... | collective-permute-start | bytes 589832 | tf_op jit(solution)/shard_map/ppermute | solution.py:39
  112.3 6.9 %collective-permute-start.15 = (bf16[256,384]{1,0:T(8,128)(2,1)S(1)}, bf16[256,384]{1,0:T(8,128)(2,1)S(1)}, u32[]{:S(2)}, u32[]{:S(2)}) collective-permute-start(bf16[256,384]{1,0:T(8,128)(2,1)S(1)} %get-tuple-element.27), channel_id=1, source_target_pairs={{17,0},{16,1},{19,2},{18,3},{21,4},{20,5},{23,6},{22,7},{25,8},{24... | collective-permute-start | bytes 589832 | tf_op jit(solution)/shard_map/ppermute | solution.py:39
  121.4 7.1 %collective-permute-start.25 = (bf16[256,256]{1,0:T(8,128)(2,1)S(1)}, bf16[256,256]{1,0:T(8,128)(2,1)S(1)}, u32[]{:S(2)}, u32[]{:S(2)}) collective-permute-start(bf16[256,256]{1,0:T(8,128)(2,1)S(1)} %get-tuple-element.31), channel_id=1, source_target_pairs={{8,0},{9,1},{10,2},{11,3},{12,4},{13,5},{14,6},{15,7},{0,8},{1,9},... | collective-permute-start | bytes 393224 | tf_op jit(solution)/shard_map/ppermute | solution.py:39
  128.5 8.8 %collective-permute-start.26 = (bf16[512,256]{1,0:T(8,128)(2,1)S(1)}, bf16[512,256]{1,0:T(8,128)(2,1)S(1)}, u32[]{:S(2)}, u32[]{:S(2)}) collective-permute-start(bf16[512,256]{1,0:T(8,128)(2,1)S(1)} %constant_dynamic-update-slice_fusion.refs_2_), channel_id=1, source_target_pairs={{7,0},{0,1},{1,2},{2,3},{3,4},{4,5},{5,6},{6,7},{15,8},{8,9},{9,10... | collective-permute-start | bytes 786440 | tf_op jit(solution)/shard_map/ppermute | solution.py:39
  130.1 7.2 %collective-permute-start.30 = (bf16[512,256]{1,0:T(8,128)(2,1)S(1)}, bf16[512,256]{1,0:T(8,128)(2,1)S(1)}, u32[]{:S(2)}, u32[]{:S(2)}) collective-permute-start(bf16[512,256]{1,0:T(8,128)(2,1)S(1)} %constant_dynamic-update-slice_fusion.refs_2_), channel_id=1, source_target_pairs={{1,0},{2,1},{3,2},{4,3},{5,4},{6,5},{7,6},{0,7},{9,8},{10,9},{11,1... | collective-permute-start | bytes 786440 | tf_op jit(solution)/shard_map/ppermute | solution.py:39
  137.3 7.8 %collective-permute-start.27 = (bf16[512,256]{1,0:T(8,128)(2,1)S(1)}, bf16[512,256]{1,0:T(8,128)(2,1)S(1)}, u32[]{:S(2)}, u32[]{:S(2)}) collective-permute-start(bf16[512,256]{1,0:T(8,128)(2,1)S(1)} %collective-permute-done.26.refs_2_), channel_id=1, source_target_pairs={{7,0},{0,1},{1,2},{2,3},{3,4},{4,5},{5,6},{6,7},{15,8},{8,9},{9,10... | collective-permute-start | bytes 786440 | tf_op jit(solution)/shard_map/ppermute | solution.py:39
  137.3 7.8 %collective-permute-start.31 = (bf16[512,256]{1,0:T(8,128)(2,1)S(1)}, bf16[512,256]{1,0:T(8,128)(2,1)S(1)}, u32[]{:S(2)}, u32[]{:S(2)}) collective-permute-start(bf16[512,256]{1,0:T(8,128)(2,1)S(1)} %collective-permute-done.30.refs_3_), channel_id=1, source_target_pairs={{1,0},{2,1},{3,2},{4,3},{5,4},{6,5},{7,6},{0,7},{9,8},{10,9},{11,1... | collective-permute-start | bytes 786440 | tf_op jit(solution)/shard_map/ppermute | solution.py:39
  145.1 15.5 %collective-permute-start.28 = (bf16[512,256]{1,0:T(8,128)(2,1)S(1)}, bf16[512,256]{1,0:T(8,128)(2,1)S(1)}, u32[]{:S(2)}, u32[]{:S(2)}) collective-permute-start(bf16[512,256]{1,0:T(8,128)(2,1)S(1)} %collective-permute-done.27.refs_2_), channel_id=1, source_target_pairs={{7,0},{0,1},{1,2},{2,3},{3,4},{4,5},{5,6},{6,7},{15,8},{8,9},{9,10... | collective-permute-start | bytes 786440 | tf_op jit(solution)/shard_map/ppermute | solution.py:39
  145.1 15.6 %collective-permute-start.32 = (bf16[512,256]{1,0:T(8,128)(2,1)S(1)}, bf16[512,256]{1,0:T(8,128)(2,1)S(1)}, u32[]{:S(2)}, u32[]{:S(2)}) collective-permute-start(bf16[512,256]{1,0:T(8,128)(2,1)S(1)} %collective-permute-done.31.refs_3_), channel_id=1, source_target_pairs={{1,0},{2,1},{3,2},{4,3},{5,4},{6,5},{7,6},{0,7},{9,8},{10,9},{11,1... | collective-permute-start | bytes 786440 | tf_op jit(solution)/shard_map/ppermute | solution.py:39
  160.6 15.0 %collective-permute-start.29 = (bf16[256,256]{1,0:T(8,128)(2,1)S(1)}, bf16[256,256]{1,0:T(8,128)(2,1)S(1)}, u32[]{:S(2)}, u32[]{:S(2)}) collective-permute-start(bf16[256,256]{1,0:T(8,128)(2,1)S(1)} %slice.94), channel_id=1, source_target_pairs={{7,0},{0,1},{1,2},{2,3},{3,4},{4,5},{5,6},{6,7},{15,8},{8,9},{9,10... | collective-permute-start | bytes 393224 | tf_op jit(solution)/shard_map/ppermute | solution.py:39
  160.7 14.9 %collective-permute-start.33 = (bf16[256,256]{1,0:T(8,128)(2,1)S(1)}, bf16[256,256]{1,0:T(8,128)(2,1)S(1)}, u32[]{:S(2)}, u32[]{:S(2)}) collective-permute-start(bf16[256,256]{1,0:T(8,128)(2,1)S(1)} %slice.95), channel_id=1, source_target_pairs={{1,0},{2,1},{3,2},{4,3},{5,4},{6,5},{7,6},{0,7},{9,8},{10,9},{11,1... | collective-permute-start | bytes 393224 | tf_op jit(solution)/shard_map/ppermute | solution.py:39
  169.8 11.0 %copy-start = (bf16[256,1536]{1,0:T(8,128)(2,1)S(1)}, bf16[256,1536]{1,0:T(8,128)(2,1)}, u32[]{:S(2)}) copy-start(bf16[256,1536]{1,0:T(8,128)(2,1)} %get-tuple-element.29.tokens_ref) | copy-start | bytes 2359300

commit v2 on v1

v2 whole, which is shorter than its diff:
```python
import functools
import math

import jax
import jax.numpy as jnp
from jax import lax
from jax.experimental import pallas as pl
from jax.experimental.pallas import tpu as pltpu
from jax.sharding import PartitionSpec as P

CIN = 768
C = 1536
HEADS = 8
HEAD_SIZE = 128
KW = 5
QW = 1024
QUARTER = C // 4
TOKENS = 256
ROWS = CIN // 16
KV = 2 * HEAD_SIZE
BOTH = ("dp", "seq")
LOG2E = math.log2(math.e)
F32 = jnp.float32
BF16 = jnp.bfloat16


def places():
    for dp in range(16):
        for seq in range(16):
            yield dp // 4, dp // 2 % 2, dp % 2, seq // 8, seq % 8


def index(x, y_lo, core, y_hi, z):
    return (x * 4 + y_lo * 2 + core) * 16 + y_hi * 8 + z


def receive(value, source):
    pairs = [(index(*source(*p)), index(*p)) for p in places()]
    return lax.ppermute(value, BOTH, pairs)


def from_core(x, y, c, h, z):
    return x, y, 1 - c, h, z


def from_z_pair(x, y, c, h, z):
    return x, y, c, h, z ^ 1


def from_diagonal(x, y, c, h, z):
    return x, y, 1 - c, h, z ^ 1


def from_x(step):
    return lambda x, y, c, h, z: (x ^ step, y, c, h, z)


def from_y(step):
    def source(x, y, c, h, z):
        at = (h * 2 + y + step) % 4
        return x, at % 2, c, at // 2, z

    return source


def from_y_hi(x, y, c, h, z):
    return x, y, c, 1 - h, z


def from_z(step):
    return lambda x, y, c, h, z: (x, y, c, h, (z + step) % 8)


VMEM = pl.BlockSpec(memory_space=pltpu.VMEM)
SMEM = pl.BlockSpec(memory_space=pltpu.SMEM)
ANY = pl.BlockSpec(memory_space=pl.ANY)


def params(mib):
    return pltpu.CompilerParams(vmem_limit_bytes=mib * 2**20)


def run_copies(copies, sems):
    started = [pltpu.make_async_copy(a, b, sems.at[i]) for i, (a, b) in enumerate(copies)]
    for copy in started:
        copy.start()
    for copy in started:
        copy.wait()


UNITS = ((0, None), (2, None), (6, None), (4, 0), (4, 1), (1, None), (3, None), (7, None), (5, 0), (5, 1))


def conv_kernel(at_ref, a_ref, bias_ref, *refs):
    units, outs, (w_ref, sems) = refs[:10], refs[10:12], refs[12:]
    step = pl.program_id(0)

    @pl.when(step == 0)
    def _():
        copies = []
        for (rel, core), unit in zip(UNITS, units):
            rows = 2 * ROWS if core is None else ROWS
            row = pl.multiple_of((at_ref[0] ^ rel) * (2 * ROWS) + (core or 0) * ROWS, ROWS)
            copies.append((unit, w_ref.at[:, pl.ds(row, rows), :]))
        run_copies(copies, sems)

    w = w_ref[...].reshape(KW * CIN, QUARTER)
    bias = bias_ref[...]
    even = jnp.dot(a_ref[0, :, : KW * CIN], w, preferred_element_type=F32) + bias
    odd = jnp.dot(a_ref[0, :, CIN:], w, preferred_element_type=F32) + bias
    pooled = jnp.maximum(jax.nn.gelu(even), jax.nn.gelu(odd)).astype(BF16)
    for i, out in enumerate(outs):

        @pl.when(step == i)
        def _(out=out):
            out[...] = pooled


def convolve(chip, blocks, bias, units):
    return pl.pallas_call(
        conv_kernel,
        grid=(2,),
        out_shape=[jax.ShapeDtypeStruct((TOKENS, QUARTER), BF16)] * 2,
        in_specs=[SMEM, pl.BlockSpec((1, TOKENS, 6 * CIN), lambda i: (i, 0, 0)), VMEM] + [ANY] * 10,
        out_specs=[pl.BlockSpec((TOKENS, QUARTER), lambda i: (0, 0))] * 2,
        scratch_shapes=[pltpu.VMEM((KW, CIN, QUARTER), BF16), pltpu.SemaphoreType.DMA((10,))],
        compiler_params=params(24),
        cost_estimate=pl.CostEstimate(flops=6_000_000_000, bytes_accessed=8_000_000, transcendentals=393216),
    )(chip, blocks, bias, *units)


def norm_kernel(at_ref, *refs):
    parts, gain_ref, w_ref = refs[:4], refs[4], refs[5]
    tokens_ref, normed_ref, pairs_ref = refs[6:]
    for i, part in enumerate(parts):
        column = pl.multiple_of((at_ref[1] ^ i) * QUARTER, QUARTER)
        tokens_ref[:, pl.ds(column, QUARTER)] = part[...]
    wide = tokens_ref[...].astype(F32)
    stat = jnp.mean(jnp.square(wide), axis=-1, keepdims=True)
    normed = (wide * lax.rsqrt(stat + 1e-06) * gain_ref[...]).astype(BF16)
    normed_ref[...] = normed
    pairs_ref[...] = jnp.dot(normed, w_ref[...], preferred_element_type=F32).astype(BF16)


def norm_and_pairs(at, parts, gain, weights):
    return pl.pallas_call(
        norm_kernel,
        grid=(1,),
        out_shape=[
            jax.ShapeDtypeStruct((TOKENS, C), BF16),
            jax.ShapeDtypeStruct((TOKENS, C), BF16),
            jax.ShapeDtypeStruct((TOKENS, KV), BF16),
        ],
        in_specs=[SMEM] + [VMEM] * 5 + [pl.BlockSpec((C, KV), lambda i: (0, QW // KV))],
        out_specs=[VMEM] * 3,
        compiler_params=params(20),
        cost_estimate=pl.CostEstimate(flops=2_000_000_000, bytes_accessed=3_500_000, transcendentals=0),
    )(at, *parts, gain, weights)


def query_kernel(normed_ref, w_ref, out_ref):
    queries = jnp.dot(normed_ref[...], w_ref[...], preferred_element_type=F32).astype(BF16)
    for head in range(HEADS):
        out_ref[head] = queries[:, head * HEAD_SIZE : (head + 1) * HEAD_SIZE]


def project_queries(normed, weights):
    return pl.pallas_call(
        query_kernel,
        grid=(1,),
        out_shape=jax.ShapeDtypeStruct((HEADS, TOKENS, HEAD_SIZE), BF16),
        in_specs=[VMEM, pl.BlockSpec((C, QW), lambda i: (0, 0))],
        out_specs=VMEM,
        compiler_params=params(20),
        cost_estimate=pl.CostEstimate(flops=2_000_000_000, bytes_accessed=4_500_000, transcendentals=0),
    )(normed, weights)


def attend_head(head, first, scale_ref, q_ref, kvs, old_refs, new_refs):
    scale = scale_ref[head]
    q = q_ref[head]
    lanes = (TOKENS, HEAD_SIZE)
    scores = [
        lax.dot_general(
            q, kv[:, :HEAD_SIZE], (((1,), (1,)), ((), ())), preferred_element_type=F32
        )
        for kv in kvs
    ]
    pieces = [
        [s[:, i : i + HEAD_SIZE] for i in range(0, s.shape[1], HEAD_SIZE)] for s in scores
    ]
    best = functools.reduce(jnp.maximum, [piece for group in pieces for piece in group])
    top = jnp.broadcast_to(jnp.max(best, axis=1, keepdims=True), lanes)
    if not first:
        old = old_refs[0][head]
        top = jnp.maximum(top, old)
        fade = jnp.exp2((old - top) * scale)
    total = jnp.zeros(lanes, F32)
    summed = jnp.zeros(lanes, F32)
    for group, kv in zip(pieces, kvs):
        weights = []
        for piece in group:
            e = jnp.exp2((piece - top) * scale)
            total = total + e
            weights.append(e.astype(BF16))
        summed = summed + jnp.dot(
            jnp.concatenate(weights, axis=1), kv[:, HEAD_SIZE:], preferred_element_type=F32
        )
    if not first:
        total = total + old_refs[1][head] * fade
        summed = summed + old_refs[2][head] * fade
    new_refs[0][head] = top
    new_refs[1][head] = total
    new_refs[2][head] = summed


def attend_kernel(n_blocks, first, scale_ref, q_ref, *refs):
    kvs, states = refs[:n_blocks], refs[n_blocks:]

    @pl.loop(0, HEADS, step=2)
    def _(head):
        for i in range(2):
            attend_head(head + i, first, scale_ref, q_ref, kvs, states[:3], states[-3:])


def attend(scale, queries, kvs, state):
    keys = sum(kv.shape[0] for kv in kvs)
    state = state or ()
    return pl.pallas_call(
        lambda *refs: attend_kernel(len(kvs), not state, *refs),
        out_shape=[jax.ShapeDtypeStruct((HEADS, TOKENS, HEAD_SIZE), F32)] * 3,
        in_specs=[SMEM] + [VMEM] * (1 + len(kvs) + len(state)),
        out_specs=[VMEM] * 3,
        compiler_params=params(20),
        cost_estimate=pl.CostEstimate(
            flops=24 * QW * TOKENS * keys,
            bytes_accessed=6_000_000,
            transcendentals=HEADS * TOKENS * keys,
        ),
    )(scale, queries, *kvs, *state)


def out_kernel(total_ref, sum_ref, tokens_ref, w_ref, out_ref):
    heads = []
    for head in range(HEADS):
        total = jnp.sum(total_ref[head], axis=1, keepdims=True)
        heads.append((sum_ref[head] / total).astype(BF16))
    context = jnp.concatenate(heads, axis=1)
    update = jnp.dot(context, w_ref[...], preferred_element_type=F32)
    out_ref[...] = (update + tokens_ref[...].astype(F32)).astype(BF16)


def project_out(total, summed, tokens, weights):
    return pl.pallas_call(
        out_kernel,
        out_shape=jax.ShapeDtypeStruct((TOKENS, C), BF16),
        in_specs=[VMEM] * 4,
        out_specs=VMEM,
        compiler_params=params(24),
        cost_estimate=pl.CostEstimate(flops=2_000_000_000, bytes_accessed=7_000_000, transcendentals=0),
    )(total, summed, tokens, weights)


def on_device(
    dna_features, conv_weight, conv_bias, norm_gain, query_weight, kv_weight, out_weight, head_scale
):
    dp, seq = lax.axis_index("dp"), lax.axis_index("seq")
    core, z = dp % 2, seq % 8
    quarter = z % 2 * 2 + core
    at = jnp.stack([dp, quarter]).astype(jnp.int32)

    shape = (KW, ROWS, QUARTER)
    keep = lax.dynamic_slice(conv_weight, (0, 0, quarter * QUARTER), shape)
    give = lax.dynamic_slice(conv_weight, (0, 0, (quarter ^ 1) * QUARTER), shape)
    got = receive(give, from_core)
    unit = jnp.concatenate(
        [jnp.where(core == 0, keep, got), jnp.where(core == 0, got, keep)], axis=1
    )
    x1, x3 = receive(unit, from_x(1)), receive(unit, from_x(3))
    y0 = receive(unit, from_y(1))
    x2a, x2b = receive(x3[:, :ROWS], from_x(1)), receive(x1[:, ROWS:], from_x(3))
    y1, y3 = receive(x1, from_y(-1)), receive(x3, from_y(1))
    y2a, y2b = receive(x2a, from_y(-1)), receive(x2b, from_y(1))
    units = (unit, x1, x3, x2a, x2b, y0, y1, y3, y2a, y2b)

    rows = dna_features.reshape(TOKENS, 2 * CIN)
    up = [(i, i + 1) for i in range(15)]
    before = lax.ppermute(rows[-1:], "seq", up)
    behind = lax.ppermute(rows[:1], "seq", [(j, i) for i, j in up])
    rows = jnp.concatenate([before, rows, behind], axis=0)
    rows_z = receive(rows, from_z_pair)
    rows_c = receive(rows, from_core)
    rows_d = receive(rows_z, from_core)
    far, near = (
        jnp.stack([jnp.concatenate([r[:TOKENS], r[1 : TOKENS + 1], r[2:]], axis=1) for r in pair])
        for pair in ((rows_d, rows_z), (rows_c, rows))
    )
    bias = lax.dynamic_slice(conv_bias.reshape(1, C), (0, quarter * QUARTER), (1, QUARTER))

    projections = jnp.concatenate([query_weight, kv_weight], axis=1)
    projections = lax.all_gather(projections, "dp", axis=0, tiled=True)
    out_weights = lax.all_gather(out_weight, "dp", axis=0, tiled=True)

    t_d, t_z = convolve(at[:1] // 2, far, bias, units)
    t_c, t_own = convolve(at[:1] // 2, near, bias, units)
    parts = (t_own, receive(t_c, from_core), receive(t_z, from_z_pair), receive(t_d, from_diagonal))
    tokens, normed, pairs = norm_and_pairs(at, parts, norm_gain.reshape(1, C), projections)

    queries = project_queries(normed, projections)
    scale = head_scale * (LOG2E / math.sqrt(HEAD_SIZE))

    both = jnp.concatenate([pairs, receive(pairs, from_y_hi)], axis=0)
    below, above = receive(both, from_z(-1)), receive(both, from_z(1))
    state = attend(scale, queries, [both], None)
    for step in range(3):
        if step < 2:
            coming = receive(below, from_z(-1)), receive(above, from_z(1))
        else:
            coming = receive(below[:TOKENS], from_z(-1)), receive(above[TOKENS:], from_z(1))
        state = attend(scale, queries, [below, above], state)
        below, above = coming
    state = attend(scale, queries, [below, above], state)
    encoded = project_out(state[1], state[2], tokens, out_weights)
    return tokens[None], encoded[None]


def solution(mesh):
    in_specs = (
        P("dp", "seq", None),
        P(None, "dp", None),
        P(),
        P(),
        P("dp", None),
        P("dp", None),
        P("dp", None),
        P(),
    )
    out_specs = (P("dp", "seq", None), P("dp", "seq", None))
    return jax.shard_map(
        on_device, mesh=mesh, in_specs=in_specs, out_specs=out_specs, check_vma=False
    )
```

time: 185 us -> 154 us (0.83); the launches traced: 185 us -> 151 us
  waiting for transfers between devices: 74.4 us -> 25.7 us
  between operations: 1.23 us -> 14.4 us
  Pallas kernels: 44.9 us -> 38.7 us
  starting transfers between devices: 51.6 us -> 56.3 us
  local copies, waits for them, and re-layouts: 6.61 us -> 9.71 us
    ppermute x32 -> x25, waiting for transfers between devices: 74.4 us -> 25.6 us  [receive(): return lax.ppermute(value, BOTH, pairs)]
    ppermute x32 -> x25, starting transfers between devices: 45.7 us -> 50.4 us  [receive(): return lax.ppermute(value, BOTH, pairs)]
    pallas_call x8 -> x9, Pallas kernels: 41 us -> 36.7 us  [the longest x5 23.3 us: attend(): pl.pallas_call(lambda *refs: attend_kernel(len(kvs), not state, *refs), o...]
    unnamed x10 -> x14, local copies, waits for them, and re-layouts: 0.78 us -> 4.86 us
    pallas_call x1, Pallas kernels: 3.86 us -> 1.96 us  [project_out(): pl.pallas_call(out_kernel, out_shape=jax.ShapeDtypeStruct((TOKENS, C), BF...]
  transfers between devices with their start and end apart: 34 -> 29, of which waited for: 13 -> 10; matrix products, arithmetic and copies ran while one was open for 6% -> 7% of each run, Pallas kernels for 18% -> 24%
where the time goes in v2:
time: 154 us; the launch traced here: 151 us
  starting transfers between devices  56.3 us (37%)
  Pallas kernels  38.7 us (25%)
  waiting for transfers between devices  25.7 us (17%)
  between operations  14.4 us (9%)
  local copies, waits for them, and re-layouts  9.71 us (6%)
  other arithmetic  6.28 us (4%)
    ppermute x25, starting transfers between devices, receive(): return lax.ppermute(value, BOTH, pairs)  50.4 us
    ppermute x25, waiting for transfers between devices, receive(): return lax.ppermute(value, BOTH, pairs)  25.6 us
    pallas_call x5, Pallas kernels, attend(): pl.pallas_call(lambda *refs: attend_kernel(len(kvs), not state, *refs), o...  23.3 us
    pallas_call x2, Pallas kernels, convolve(): pl.pallas_call(conv_kernel, grid=(2,), out_shape=[jax.ShapeDtypeStruct((T...  10.6 us
    unnamed x14, local copies, waits for them, and re-layouts  4.86 us
    ppermute x1, starting transfers between devices, on_device(): before = lax.ppermute(rows[-1:], 'seq', up)  4.55 us
    another operation x5, other arithmetic, on_device(): jnp.stack([jnp.concatenate([r[:TOKENS], r[1:TOKENS + 1], r[2:]], axis=1)...  3.3 us
  transfers between devices with their start and end apart: 29, of which 10 were waited for; matrix products, arithmetic and copies ran while one was open for 7% of the time, Pallas kernels for 24%

profile of v2, /device:TPU:2, one launch (start us, length us, event | category | flops | bytes accessed | tf_op | source)
XLA Modules:
  0.0 151.1 jit_solution(3478747249156445770)
XLA Ops:
  7.2 1.7 %pad_maximum_fusion.6 = bf16[96,1280]{1,0:T(8,128)(2,1)} fusion(bf16[96,256]{1,0:T(8,128)(2,1)} %param.13, bf16[96,1024]{1,0:T(8,128)(2,1)} %param.12), kind=kLoop, calls=%fused_computation.12 | loop fusion | flops 491520 | bytes 491520 | tf_op jit(solution)/shard_map/concatenate | solution.py:300
  8.9 0.0 all-gather.5.cloned.1.call-start
  9.0 0.7 slice_bitcast_fusion.1
  9.7 1.3 collective-permute-start.1
  11.0 4.5 %collective-permute-start = (bf16[1,1536]{1,0:T(2,128)(2,1)S(1)}, bf16[1,1536]{1,0:T(2,128)(2,1)S(1)}, u32[]{:S(2)}, u32[]{:S(2)}) collective-permute-start(bf16[1,1536]{1,0:T(2,128)(2,1)S(1)} %bitcast.20), channel_id=1, source_target_pairs={{0,1},{1,2},{2,3},{3,4},{4,5},{5,6},{6,7},{7,8},{8,9},{9,10},{10,1... | collective-permute-start | bytes 9224 | tf_op jit(solution)/shard_map/ppermute | solution.py:288
  15.6 0.9 constant_dynamic-slice_fusion
  16.6 0.1 collective-permute-start.3
  16.7 0.1 pad_add_fusion.at_ref
  16.8 1.4 reshape.18
  18.1 0.8 dynamic-slice.3
  18.9 0.7 reshape.19.refs_4_
  19.6 0.2 pad_maximum_fusion.4
  19.8 0.6 collective-permute-start.2
  20.4 1.9 %collective-permute-start.14 = (bf16[258,1536]{1,0:T(8,128)(2,1)S(1)}, bf16[258,1536]{1,0:T(8,128)(2,1)S(1)}, u32[]{:S(2)}, u32[]{:S(2)}) collective-permute-start(bf16[258,1536]{1,0:T(8,128)(2,1)S(1)} %pad_maximum_fusion.4), channel_id=1, source_target_pairs={{1,0},{0,1},{3,2},{2,3},{5,4},{4,5},{7,6},{6,7},{9,8},{8,9},{11,10... | collective-permute-start | bytes 2377736 | tf_op jit(solution)/shard_map/ppermute | solution.py:39
  22.3 1.0 broadcast_select_fusion.1
  23.4 0.6 collective-permute-start.4
  24.0 2.2 %collective-permute-start.5 = (bf16[5,96,384]{2,1,0:T(8,128)(2,1)S(1)}, bf16[5,96,384]{2,1,0:T(8,128)(2,1)S(1)}, u32[]{:S(2)}, u32[]{:S(2)}) collective-permute-start(bf16[5,96,384]{2,1,0:T(8,128)(2,1)S(1)} %pad_maximum_fusion.5.refs_0_), channel_id=1, source_target_pairs={{192,0},{193,1},{194,2},{195,3},{196,4},{197,5},{198,6},{199,7},{2... | collective-permute-start | bytes 1105928 | tf_op jit(solution)/shard_map/ppermute | solution.py:39
  26.2 1.9 %fusion.1 = bf16[1,256,4608]{2,1,0:T(8,128)(2,1)S(1)} fusion(bf16[1,1536]{1,0:T(2,128)(2,1)S(1)} %collective-permute-done.1, bf16[256,1536]{1,0:T(8,128)(2,1)S(1)} %reshape.18, bf16[1,1536]{1,0:T(2,128)(2,1)S(1)} %collective-permute-done), kind=kLoop, calls=%fused_computation.4 | loop fusion | flops 11796480 | bytes 3151872 | tf_op jit(solution)/shard_map/stack | solution.py:295
  28.1 8.6 %collective-permute-start.8 = (bf16[5,96,384]{2,1,0:T(8,128)(2,1)S(1)}, bf16[5,96,384]{2,1,0:T(8,128)(2,1)S(1)}, u32[]{:S(2)}, u32[]{:S(2)}) collective-permute-start(bf16[5,96,384]{2,1,0:T(8,128)(2,1)S(1)} %pad_maximum_fusion.5.refs_0_), channel_id=1, source_target_pairs={{32,0},{33,1},{34,2},{35,3},{36,4},{37,5},{38,6},{39,7},{40,8},{41... | collective-permute-start | bytes 1105928 | tf_op jit(solution)/shard_map/ppermute | solution.py:39
  36.7 5.8 %collective-permute-done.5.refs_2_ = bf16[5,96,384]{2,1,0:T(8,128)(2,1)S(1)} collective-permute-done((bf16[5,96,384]{2,1,0:T(8,128)(2,1)S(1)}, bf16[5,96,384]{2,1,0:T(8,128)(2,1)S(1)}, u32[]{:S(2)}, u32[]{:S(2)}) %collective-permute-start.5) | collective-permute-done | bytes 368672 | tf_op jit(solution)/shard_map/ppermute | solution.py:39
  42.5 0.1 collective-permute-start.6
  42.6 2.5 %collective-permute-start.7 = (bf16[5,48,384]{2,1,0:T(8,128)(2,1)S(1)}, bf16[5,48,384]{2,1,0:T(8,128)(2,1)S(1)}, u32[]{:S(2)}, u32[]{:S(2)}) collective-permute-start(bf16[5,48,384]{2,1,0:T(8,128)(2,1)S(1)} %slice.82), channel_id=1, source_target_pairs={{192,0},{193,1},{194,2},{195,3},{196,4},{197,5},{198,6},{199,7},{2... | collective-permute-start | bytes 552968 | tf_op jit(solution)/shard_map/ppermute | solution.py:39
  45.1 1.4 collective-permute-start.9
  46.5 0.3 fusion.5
  46.9 0.2 maximum_bitcast_fusion
  47.0 0.4 pad_maximum_fusion.a_ref
  47.5 7.1 %collective-permute-start.10 = (bf16[5,96,384]{2,1,0:T(8,128)(2,1)S(1)}, bf16[5,96,384]{2,1,0:T(8,128)(2,1)S(1)}, u32[]{:S(2)}, u32[]{:S(2)}) collective-permute-start(bf16[5,96,384]{2,1,0:T(8,128)(2,1)S(1)} %collective-permute-done.5.refs_2_), channel_id=1, source_target_pairs={{32,0},{33,1},{34,2},{35,3},{36,4},{37,5},{38,6},{39,7},{40,8},{41... | collective-permute-start | bytes 1105928 | tf_op jit(solution)/shard_map/ppermute | solution.py:39
  54.6 6.5 %collective-permute-start.12 = (bf16[5,48,384]{2,1,0:T(8,128)(2,1)S(1)}, bf16[5,48,384]{2,1,0:T(8,128)(2,1)S(1)}, u32[]{:S(2)}, u32[]{:S(2)}) collective-permute-start(bf16[5,48,384]{2,1,0:T(8,128)(2,1)S(1)} %collective-permute-done.7.refs_4_), channel_id=1, source_target_pairs={{32,0},{33,1},{34,2},{35,3},{36,4},{37,5},{38,6},{39,7},{40,8},{41... | collective-permute-start | bytes 552968 | tf_op jit(solution)/shard_map/ppermute | solution.py:39
  61.1 0.3 fusion.4
  61.4 0.4 collective-permute-done.9.refs_6_
  61.8 1.2 collective-permute-done.10.refs_7_
  63.0 2.8 %collective-permute-done.11.refs_8_ = bf16[5,48,384]{2,1,0:T(8,128)(2,1)S(1)} collective-permute-done((bf16[5,48,384]{2,1,0:T(8,128)(2,1)S(1)}, bf16[5,48,384]{2,1,0:T(8,128)(2,1)S(1)}, u32[]{:S(2)}, u32[]{:S(2)}) %collective-permute-start.11) | collective-permute-done | bytes 184352 | tf_op jit(solution)/shard_map/ppermute | solution.py:39
  65.8 0.3 collective-permute-done.12.refs_9_
  66.0 5.3 %shard_map.95 = (bf16[256,384]{1,0:T(8,128)(2,1)S(1)}, bf16[256,384]{1,0:T(8,128)(2,1)S(1)}) custom-call(s32[1]{0:T(128)S(6)} %select_n.43.at_ref, bf16[2,256,4608]{2,1,0:T(8,128)(2,1)S(1)} %pad_maximum_fusion.a_ref, f32[1,384]{1,0:T(1,128)S(1)} %dynamic_slice.9.bias_ref, bf16[5,96,384]{2,1,0:T(8,128)(2,1)S(1)} %pad_maximum_fusion.5.refs_0_, ...), custom_call_target="tpu_custom_call" | custom-call | flops 6000000000 | bytes 8000000 | tf_op jit(solution)/shard_map/pallas_call | solution.py:120
  71.3 0.1 collective-permute-start.13
  71.4 0.3 fusion.3
  71.8 0.4 maximum_bitcast_fusion.1
  72.1 0.4 pad_maximum_fusion.1.a_ref
  72.6 5.3 %shard_map.96 = (bf16[256,384]{1,0:T(8,128)(2,1)S(1)}, bf16[256,384]{1,0:T(8,128)(2,1)S(1)}) custom-call(s32[1]{0:T(128)S(6)} %select_n.43.at_ref, bf16[2,256,4608]{2,1,0:T(8,128)(2,1)S(1)} %pad_maximum_fusion.1.a_ref, f32[1,384]{1,0:T(1,128)S(1)} %dynamic_slice.9.bias_ref, bf16[5,96,384]{2,1,0:T(8,128)(2,1)S(1)} %pad_maximum_fusion.5.refs_0_, ...), custom_call_target="tpu_custom_call" | custom-call | flops 6000000000 | bytes 8000000 | tf_op jit(solution)/shard_map/pallas_call | solution.py:120
  77.9 1.5 %collective-permute-start.16 = (bf16[256,384]{1,0:T(8,128)(2,1)S(1)}, bf16[256,384]{1,0:T(8,128)(2,1)S(1)}, u32[]{:S(2)}, u32[]{:S(2)}) collective-permute-start(bf16[256,384]{1,0:T(8,128)(2,1)S(1)} %get-tuple-element.25), channel_id=1, source_target_pairs={{1,0},{0,1},{3,2},{2,3},{5,4},{4,5},{7,6},{6,7},{9,8},{8,9},{11,10... | collective-permute-start | bytes 589832 | tf_op jit(solution)/shard_map/ppermute | solution.py:39
  79.5 0.4 collective-permute-start.17
  79.9 5.8 %collective-permute-done.16.refs_2_ = bf16[256,384]{1,0:T(8,128)(2,1)S(1)} collective-permute-done((bf16[256,384]{1,0:T(8,128)(2,1)S(1)}, bf16[256,384]{1,0:T(8,128)(2,1)S(1)}, u32[]{:S(2)}, u32[]{:S(2)}) %collective-permute-start.16) | collective-permute-done | bytes 196640 | tf_op jit(solution)/shard_map/ppermute | solution.py:39
  85.7 3.4 %collective-permute-done.17.refs_3_ = bf16[256,384]{1,0:T(8,128)(2,1)S(1)} collective-permute-done((bf16[256,384]{1,0:T(8,128)(2,1)S(1)}, bf16[256,384]{1,0:T(8,128)(2,1)S(1)}, u32[]{:S(2)}, u32[]{:S(2)}) %collective-permute-start.17) | collective-permute-done | bytes 196640 | tf_op jit(solution)/shard_map/ppermute | solution.py:39
  89.1 2.2 %copy-done = bf16[1536,1280]{1,0:T(8,128)(2,1)S(1)} copy-done((bf16[1536,1280]{1,0:T(8,128)(2,1)S(1)}, bf16[1536,1280]{1,0:T(8,128)(2,1)}, u32[]{:S(2)}) %copy-start) | copy-done | bytes 3932184
  91.3 1.9 %shard_map.97 = (bf16[256,1536]{1,0:T(8,128)(2,1)}, bf16[256,1536]{1,0:T(8,128)(2,1)S(1)}, bf16[256,256]{1,0:T(8,128)(2,1)S(1)}) custom-call(s32[2]{0:T(128)S(1)} %pad_add_fusion.at_ref, bf16[256,384]{1,0:T(8,128)(2,1)S(1)} %get-tuple-element.23.refs_0_, bf16[256,384]{1,0:T(8,128)(2,1)S(1)} %collective-permute-done.13.refs_1_, ...), custom_call_target="tpu_custom_call" | custom-call | flops 2000000000 | bytes 3500000 | tf_op jit(solution)/shard_map/pallas_call | solution.py:146
  93.2 3.7 %collective-permute-start.18 = (bf16[256,256]{1,0:T(8,128)(2,1)S(1)}, bf16[256,256]{1,0:T(8,128)(2,1)S(1)}, u32[]{:S(2)}, u32[]{:S(2)}) collective-permute-start(bf16[256,256]{1,0:T(8,128)(2,1)S(1)} %get-tuple-element.29), channel_id=1, source_target_pairs={{8,0},{9,1},{10,2},{11,3},{12,4},{13,5},{14,6},{15,7},{0,8},{1,9},... | collective-permute-start | bytes 393224 | tf_op jit(solution)/shard_map/ppermute | solution.py:39
  96.9 1.0 shard_map.98.refs_1_
  97.9 3.2 %collective-permute-done.18 = bf16[256,256]{1,0:T(8,128)(2,1)S(1)} collective-permute-done((bf16[256,256]{1,0:T(8,128)(2,1)S(1)}, bf16[256,256]{1,0:T(8,128)(2,1)S(1)}, u32[]{:S(2)}, u32[]{:S(2)}) %collective-permute-start.18) | collective-permute-done | bytes 131104 | tf_op jit(solution)/shard_map/ppermute | solution.py:39
  101.1 1.5 %collective-permute-start.19 = (bf16[512,256]{1,0:T(8,128)(2,1)S(1)}, bf16[512,256]{1,0:T(8,128)(2,1)S(1)}, u32[]{:S(2)}, u32[]{:S(2)}) collective-permute-start(bf16[512,256]{1,0:T(8,128)(2,1)S(1)} %constant_dynamic-update-slice_fusion.refs_2_), channel_id=1, source_target_pairs={{7,0},{0,1},{1,2},{2,3},{3,4},{4,5},{5,6},{6,7},{15,8},{8,9},{9,10... | collective-permute-start | bytes 786440 | tf_op jit(solution)/shard_map/ppermute | solution.py:39
  102.6 1.8 %collective-permute-start.23 = (bf16[512,256]{1,0:T(8,128)(2,1)S(1)}, bf16[512,256]{1,0:T(8,128)(2,1)S(1)}, u32[]{:S(2)}, u32[]{:S(2)}) collective-permute-start(bf16[512,256]{1,0:T(8,128)(2,1)S(1)} %constant_dynamic-update-slice_fusion.refs_2_), channel_id=1, source_target_pairs={{1,0},{2,1},{3,2},{4,3},{5,4},{6,5},{7,6},{0,7},{9,8},{10,9},{11,1... | collective-permute-start | bytes 786440 | tf_op jit(solution)/shard_map/ppermute | solution.py:39
  104.4 3.6 %shard_map.99 = (f32[8,256,128]{2,1,0:T(8,128)S(1)}, f32[8,256,128]{2,1,0:T(8,128)S(1)}, f32[8,256,128]{2,1,0:T(8,128)S(1)}) custom-call(f32[8]{0:T(128)S(1)} %broadcast_multiply_fusion.refs_0_, bf16[8,256,128]{2,1,0:T(8,128)(2,1)S(1)} %shard_map.98.refs_1_, bf16[512,256]{1,0:T(8,128)(2,1)S(1)} %constant_dynamic-update-slice_fusion.refs_2_), custom_call_target="tpu_custom_call" | custom-call | flops 3221225472 | bytes 6000000 | tf_op jit(solution)/shard_map/pallas_call | solution.py:229
  108.0 2.5 %collective-permute-done.19.refs_2_ = bf16[512,256]{1,0:T(8,128)(2,1)S(1)} collective-permute-done((bf16[512,256]{1,0:T(8,128)(2,1)S(1)}, bf16[512,256]{1,0:T(8,128)(2,1)S(1)}, u32[]{:S(2)}, u32[]{:S(2)}) %collective-permute-start.19) | collective-permute-done | bytes 262176 | tf_op jit(solution)/shard_map/ppermute | solution.py:39
  110.5 0.3 collective-permute-start.20
  110.9 2.9 %collective-permute-start.24 = (bf16[512,256]{1,0:T(8,128)(2,1)S(1)}, bf16[512,256]{1,0:T(8,128)(2,1)S(1)}, u32[]{:S(2)}, u32[]{:S(2)}) collective-permute-start(bf16[512,256]{1,0:T(8,128)(2,1)S(1)} %collective-permute-done.23.refs_3_), channel_id=1, source_target_pairs={{1,0},{2,1},{3,2},{4,3},{5,4},{6,5},{7,6},{0,7},{9,8},{10,9},{11,1... | collective-permute-start | bytes 786440 | tf_op jit(solution)/shard_map/ppermute | solution.py:39
  113.8 5.0 %shard_map.100 = (f32[8,256,128]{2,1,0:T(8,128)S(1)}, f32[8,256,128]{2,1,0:T(8,128)S(1)}, f32[8,256,128]{2,1,0:T(8,128)S(1)}) custom-call(f32[8]{0:T(128)S(1)} %broadcast_multiply_fusion.refs_0_, bf16[8,256,128]{2,1,0:T(8,128)(2,1)S(1)} %shard_map.98.refs_1_, bf16[512,256]{1,0:T(8,128)(2,1)S(1)} %collective-permute-done.19.refs_2_, ...), custom_call_target="tpu_custom_call" | custom-call | flops 6442450944 | bytes 6000000 | tf_op jit(solution)/shard_map/pallas_call | solution.py:229
  118.8 0.3 collective-permute-done.20.refs_2_
  119.1 3.2 %collective-permute-start.25 = (bf16[512,256]{1,0:T(8,128)(2,1)S(1)}, bf16[512,256]{1,0:T(8,128)(2,1)S(1)}, u32[]{:S(2)}, u32[]{:S(2)}) collective-permute-start(bf16[512,256]{1,0:T(8,128)(2,1)S(1)} %collective-permute-done.24.refs_3_), channel_id=1, source_target_pairs={{1,0},{2,1},{3,2},{4,3},{5,4},{6,5},{7,6},{0,7},{9,8},{10,9},{11,1... | collective-permute-start | bytes 786440 | tf_op jit(solution)/shard_map/ppermute | solution.py:39
  122.3 5.0 %shard_map.101 = (f32[8,256,128]{2,1,0:T(8,128)S(1)}, f32[8,256,128]{2,1,0:T(8,128)S(1)}, f32[8,256,128]{2,1,0:T(8,128)S(1)}) custom-call(f32[8]{0:T(128)S(1)} %broadcast_multiply_fusion.refs_0_, bf16[8,256,128]{2,1,0:T(8,128)(2,1)S(1)} %shard_map.98.refs_1_, bf16[512,256]{1,0:T(8,128)(2,1)S(1)} %collective-permute-done.20.refs_2_, ...), custom_call_target="tpu_custom_call" | custom-call | flops 6442450944 | bytes 6000000 | tf_op jit(solution)/shard_map/pallas_call | solution.py:229
  127.4 0.1 collective-permute-start.22
  127.5 3.3 %collective-permute-start.26 = (bf16[256,256]{1,0:T(8,128)(2,1)S(1)}, bf16[256,256]{1,0:T(8,128)(2,1)S(1)}, u32[]{:S(2)}, u32[]{:S(2)}) collective-permute-start(bf16[256,256]{1,0:T(8,128)(2,1)S(1)} %slice.90), channel_id=1, source_target_pairs={{1,0},{2,1},{3,2},{4,3},{5,4},{6,5},{7,6},{0,7},{9,8},{10,9},{11,1... | collective-permute-start | bytes 393224 | tf_op jit(solution)/shard_map/ppermute | solution.py:39
  130.8 5.0 %shard_map.102 = (f32[8,256,128]{2,1,0:T(8,128)S(1)}, f32[8,256,128]{2,1,0:T(8,128)S(1)}, f32[8,256,128]{2,1,0:T(8,128)S(1)}) custom-call(f32[8]{0:T(128)S(1)} %broadcast_multiply_fusion.refs_0_, bf16[8,256,128]{2,1,0:T(8,128)(2,1)S(1)} %shard_map.98.refs_1_, bf16[512,256]{1,0:T(8,128)(2,1)S(1)} %collective-permute-done.21.refs_2_, ...), custom_call_target="tpu_custom_call" | custom-call | flops 6442450944 | bytes 6000000 | tf_op jit(solution)/shard_map/pallas_call | solution.py:229
  135.8 4.6 %shard_map.103 = (f32[8,256,128]{2,1,0:T(8,128)}, f32[8,256,128]{2,1,0:T(8,128)S(1)}, f32[8,256,128]{2,1,0:T(8,128)S(1)}) custom-call(f32[8]{0:T(128)S(1)} %broadcast_multiply_fusion.refs_0_, bf16[8,256,128]{2,1,0:T(8,128)(2,1)S(1)} %shard_map.98.refs_1_, bf16[256,256]{1,0:T(8,128)(2,1)S(1)} %collective-permute-done.22.refs_2_, ...), custom_call_target="tpu_custom_call" | custom-call | flops 3221225472 | bytes 6000000 | tf_op jit(solution)/shard_map/pallas_call | solution.py:229
  140.4 1.9 %copy-done.2 = bf16[1024,1536]{1,0:T(8,128)(2,1)S(1)} copy-done((bf16[1024,1536]{1,0:T(8,128)(2,1)S(1)}, bf16[1024,1536]{1,0:T(8,128)(2,1)}, u32[]{:S(2)}) %copy-start.2) | copy-done | bytes 3145752
  142.3 2.0 %shard_map.104 = bf16[256,1536]{1,0:T(8,128)(2,1)} custom-call(f32[8,256,128]{2,1,0:T(8,128)S(1)} %get-tuple-element.42.total_ref, f32[8,256,128]{2,1,0:T(8,128)S(1)} %get-tuple-element.43.sum_ref, bf16[256,1536]{1,0:T(8,128)(2,1)S(1)} %copy-done.3, bf16[1024,1536]{1,0:T(8,128)(2,1)S(1)} %copy-done.2), custom_call_target="tpu_custom_call" | custom-call | flops 2000000000 | bytes 7000000 | tf_op jit(solution)/shard_map/pallas_call | solution.py:254
  (44 shorter events, 0.3 us)
Async XLA Ops:
  7.2 82.0 %all-gather.3.cloned.1.call-start = ((), (), s32[]{:S(2)}) async-start(), calls=%async_computation | async-start | bytes 4177920 | tf_op jit(solution)/shard_map/all_gather | solution.py:301
  8.9 131.5 %all-gather.5.cloned.1.call-start = ((), (), s32[]{:S(2)}) async-start(), calls=%async_computation.1 | async-start | bytes 3342336 | tf_op jit(solution)/shard_map/all_gather | solution.py:302
  9.7 9.9 %collective-permute-start.1 = (bf16[1,1536]{1,0:T(2,128)(2,1)S(1)}, bf16[1,1536]{1,0:T(2,128)(2,1)S(1)}, u32[]{:S(2)}, u32[]{:S(2)}) collective-permute-start(bf16[1,1536]{1,0:T(2,128)(2,1)S(1)} %bitcast.19), channel_id=1, source_target_pairs={{1,0},{2,1},{3,2},{4,3},{5,4},{6,5},{7,6},{8,7},{9,8},{10,9},{11,1... | collective-permute-start | bytes 9224 | tf_op jit(solution)/shard_map/ppermute | solution.py:289
  11.0 8.6 %collective-permute-start = (bf16[1,1536]{1,0:T(2,128)(2,1)S(1)}, bf16[1,1536]{1,0:T(2,128)(2,1)S(1)}, u32[]{:S(2)}, u32[]{:S(2)}) collective-permute-start(bf16[1,1536]{1,0:T(2,128)(2,1)S(1)} %bitcast.20), channel_id=1, source_target_pairs={{0,1},{1,2},{2,3},{3,4},{4,5},{5,6},{6,7},{7,8},{8,9},{9,10},{10,1... | collective-permute-start | bytes 9224 | tf_op jit(solution)/shard_map/ppermute | solution.py:288
  16.6 5.8 %collective-permute-start.3 = (bf16[5,48,384]{2,1,0:T(8,128)(2,1)S(1)}, bf16[5,48,384]{2,1,0:T(8,128)(2,1)S(1)}, u32[]{:S(2)}, u32[]{:S(2)}) collective-permute-start(bf16[5,48,384]{2,1,0:T(8,128)(2,1)S(1)} %constant_dynamic-slice_fusion), channel_id=1, source_target_pairs={{16,0},{17,1},{18,2},{19,3},{20,4},{21,5},{22,6},{23,7},{24,8},{25... | collective-permute-start | bytes 552968 | tf_op jit(solution)/shard_map/ppermute | solution.py:39
  19.8 25.3 %collective-permute-start.2 = (bf16[258,1536]{1,0:T(8,128)(2,1)S(1)}, bf16[258,1536]{1,0:T(8,128)(2,1)S(1)}, u32[]{:S(2)}, u32[]{:S(2)}) collective-permute-start(bf16[258,1536]{1,0:T(8,128)(2,1)S(1)} %pad_maximum_fusion.4), channel_id=1, source_target_pairs={{16,0},{17,1},{18,2},{19,3},{20,4},{21,5},{22,6},{23,7},{24,8},{25... | collective-permute-start | bytes 2377736 | tf_op jit(solution)/shard_map/ppermute | solution.py:39
  20.4 40.7 %collective-permute-start.14 = (bf16[258,1536]{1,0:T(8,128)(2,1)S(1)}, bf16[258,1536]{1,0:T(8,128)(2,1)S(1)}, u32[]{:S(2)}, u32[]{:S(2)}) collective-permute-start(bf16[258,1536]{1,0:T(8,128)(2,1)S(1)} %pad_maximum_fusion.4), channel_id=1, source_target_pairs={{1,0},{0,1},{3,2},{2,3},{5,4},{4,5},{7,6},{6,7},{9,8},{8,9},{11,10... | collective-permute-start | bytes 2377736 | tf_op jit(solution)/shard_map/ppermute | solution.py:39
  23.4 19.2 %collective-permute-start.4 = (bf16[5,96,384]{2,1,0:T(8,128)(2,1)S(1)}, bf16[5,96,384]{2,1,0:T(8,128)(2,1)S(1)}, u32[]{:S(2)}, u32[]{:S(2)}) collective-permute-start(bf16[5,96,384]{2,1,0:T(8,128)(2,1)S(1)} %pad_maximum_fusion.5.refs_0_), channel_id=1, source_target_pairs={{64,0},{65,1},{66,2},{67,3},{68,4},{69,5},{70,6},{71,7},{72,8},{73... | collective-permute-start | bytes 1105928 | tf_op jit(solution)/shard_map/ppermute | solution.py:39
  24.0 18.4 %collective-permute-start.5 = (bf16[5,96,384]{2,1,0:T(8,128)(2,1)S(1)}, bf16[5,96,384]{2,1,0:T(8,128)(2,1)S(1)}, u32[]{:S(2)}, u32[]{:S(2)}) collective-permute-start(bf16[5,96,384]{2,1,0:T(8,128)(2,1)S(1)} %pad_maximum_fusion.5.refs_0_), channel_id=1, source_target_pairs={{192,0},{193,1},{194,2},{195,3},{196,4},{197,5},{198,6},{199,7},{2... | collective-permute-start | bytes 1105928 | tf_op jit(solution)/shard_map/ppermute | solution.py:39
  28.1 19.4 %collective-permute-start.8 = (bf16[5,96,384]{2,1,0:T(8,128)(2,1)S(1)}, bf16[5,96,384]{2,1,0:T(8,128)(2,1)S(1)}, u32[]{:S(2)}, u32[]{:S(2)}) collective-permute-start(bf16[5,96,384]{2,1,0:T(8,128)(2,1)S(1)} %pad_maximum_fusion.5.refs_0_), channel_id=1, source_target_pairs={{32,0},{33,1},{34,2},{35,3},{36,4},{37,5},{38,6},{39,7},{40,8},{41... | collective-permute-start | bytes 1105928 | tf_op jit(solution)/shard_map/ppermute | solution.py:39
  42.5 12.1 %collective-permute-start.6 = (bf16[5,48,384]{2,1,0:T(8,128)(2,1)S(1)}, bf16[5,48,384]{2,1,0:T(8,128)(2,1)S(1)}, u32[]{:S(2)}, u32[]{:S(2)}) collective-permute-start(bf16[5,48,384]{2,1,0:T(8,128)(2,1)S(1)} %slice.81), channel_id=1, source_target_pairs={{64,0},{65,1},{66,2},{67,3},{68,4},{69,5},{70,6},{71,7},{72,8},{73... | collective-permute-start | bytes 552968 | tf_op jit(solution)/shard_map/ppermute | solution.py:39
  42.6 12.0 %collective-permute-start.7 = (bf16[5,48,384]{2,1,0:T(8,128)(2,1)S(1)}, bf16[5,48,384]{2,1,0:T(8,128)(2,1)S(1)}, u32[]{:S(2)}, u32[]{:S(2)}) collective-permute-start(bf16[5,48,384]{2,1,0:T(8,128)(2,1)S(1)} %slice.82), channel_id=1, source_target_pairs={{192,0},{193,1},{194,2},{195,3},{196,4},{197,5},{198,6},{199,7},{2... | collective-permute-start | bytes 552968 | tf_op jit(solution)/shard_map/ppermute | solution.py:39
  45.1 16.6 %collective-permute-start.9 = (bf16[5,96,384]{2,1,0:T(8,128)(2,1)S(1)}, bf16[5,96,384]{2,1,0:T(8,128)(2,1)S(1)}, u32[]{:S(2)}, u32[]{:S(2)}) collective-permute-start(bf16[5,96,384]{2,1,0:T(8,128)(2,1)S(1)} %collective-permute-done.4.refs_1_), channel_id=1, source_target_pairs={{40,0},{41,1},{42,2},{43,3},{44,4},{45,5},{46,6},{47,7},{32,8},{33... | collective-permute-start | bytes 1105928 | tf_op jit(solution)/shard_map/ppermute | solution.py:39
  47.5 15.5 %collective-permute-start.10 = (bf16[5,96,384]{2,1,0:T(8,128)(2,1)S(1)}, bf16[5,96,384]{2,1,0:T(8,128)(2,1)S(1)}, u32[]{:S(2)}, u32[]{:S(2)}) collective-permute-start(bf16[5,96,384]{2,1,0:T(8,128)(2,1)S(1)} %collective-permute-done.5.refs_2_), channel_id=1, source_target_pairs={{32,0},{33,1},{34,2},{35,3},{36,4},{37,5},{38,6},{39,7},{40,8},{41... | collective-permute-start | bytes 1105928 | tf_op jit(solution)/shard_map/ppermute | solution.py:39
  54.6 11.2 %collective-permute-start.11 = (bf16[5,48,384]{2,1,0:T(8,128)(2,1)S(1)}, bf16[5,48,384]{2,1,0:T(8,128)(2,1)S(1)}, u32[]{:S(2)}, u32[]{:S(2)}) collective-permute-start(bf16[5,48,384]{2,1,0:T(8,128)(2,1)S(1)} %collective-permute-done.6.refs_3_), channel_id=1, source_target_pairs={{40,0},{41,1},{42,2},{43,3},{44,4},{45,5},{46,6},{47,7},{32,8},{33... | collective-permute-start | bytes 552968 | tf_op jit(solution)/shard_map/ppermute | solution.py:39
  54.6 11.4 %collective-permute-start.12 = (bf16[5,48,384]{2,1,0:T(8,128)(2,1)S(1)}, bf16[5,48,384]{2,1,0:T(8,128)(2,1)S(1)}, u32[]{:S(2)}, u32[]{:S(2)}) collective-permute-start(bf16[5,48,384]{2,1,0:T(8,128)(2,1)S(1)} %collective-permute-done.7.refs_4_), channel_id=1, source_target_pairs={{32,0},{33,1},{34,2},{35,3},{36,4},{37,5},{38,6},{39,7},{40,8},{41... | collective-permute-start | bytes 552968 | tf_op jit(solution)/shard_map/ppermute | solution.py:39
  61.1 10.3 %collective-permute-start.15 = (bf16[258,1536]{1,0:T(8,128)(2,1)S(1)}, bf16[258,1536]{1,0:T(8,128)(2,1)S(1)}, u32[]{:S(2)}, u32[]{:S(2)}) collective-permute-start(bf16[258,1536]{1,0:T(8,128)(2,1)S(1)} %collective-permute-done.14), channel_id=1, source_target_pairs={{16,0},{17,1},{18,2},{19,3},{20,4},{21,5},{22,6},{23,7},{24,8},{25... | collective-permute-start | bytes 2377736 | tf_op jit(solution)/shard_map/ppermute | solution.py:39
  71.3 8.5 %collective-permute-start.13 = (bf16[256,384]{1,0:T(8,128)(2,1)S(1)}, bf16[256,384]{1,0:T(8,128)(2,1)S(1)}, u32[]{:S(2)}, u32[]{:S(2)}) collective-permute-start(bf16[256,384]{1,0:T(8,128)(2,1)S(1)} %get-tuple-element.24), channel_id=1, source_target_pairs={{16,0},{17,1},{18,2},{19,3},{20,4},{21,5},{22,6},{23,7},{24,8},{25... | collective-permute-start | bytes 589832 | tf_op jit(solution)/shard_map/ppermute | solution.py:39
  72.6 7.3 %copy-start.4 = (f32[8]{0:T(128)S(1)}, f32[8]{0:T(128)}, u32[]{:S(2)}) copy-start(f32[8]{0:T(128)} %param.15) | copy-start | bytes 100
  77.9 7.8 %collective-permute-start.16 = (bf16[256,384]{1,0:T(8,128)(2,1)S(1)}, bf16[256,384]{1,0:T(8,128)(2,1)S(1)}, u32[]{:S(2)}, u32[]{:S(2)}) collective-permute-start(bf16[256,384]{1,0:T(8,128)(2,1)S(1)} %get-tuple-element.25), channel_id=1, source_target_pairs={{1,0},{0,1},{3,2},{2,3},{5,4},{4,5},{7,6},{6,7},{9,8},{8,9},{11,10... | collective-permute-start | bytes 589832 | tf_op jit(solution)/shard_map/ppermute | solution.py:39
  79.5 9.7 %collective-permute-start.17 = (bf16[256,384]{1,0:T(8,128)(2,1)S(1)}, bf16[256,384]{1,0:T(8,128)(2,1)S(1)}, u32[]{:S(2)}, u32[]{:S(2)}) collective-permute-start(bf16[256,384]{1,0:T(8,128)(2,1)S(1)} %get-tuple-element.26), channel_id=1, source_target_pairs={{17,0},{16,1},{19,2},{18,3},{21,4},{20,5},{23,6},{22,7},{25,8},{24... | collective-permute-start | bytes 589832 | tf_op jit(solution)/shard_map/ppermute | solution.py:39
  89.1 2.2 %copy-start = (bf16[1536,1280]{1,0:T(8,128)(2,1)S(1)}, bf16[1536,1280]{1,0:T(8,128)(2,1)}, u32[]{:S(2)}) copy-start(bf16[1536,1280]{1,0:T(8,128)(2,1)} %all-gather.3.cloned.1.call-done.refs_5_.w_ref) | copy-start | bytes 11796484
  91.3 5.6 %copy-start.1 = (bf16[1536,1280]{1,0:T(8,128)(2,1)S(1)}, bf16[1536,1280]{1,0:T(8,128)(2,1)}, u32[]{:S(2)}) copy-start(bf16[1536,1280]{1,0:T(8,128)(2,1)} %all-gather.3.cloned.1.call-done.refs_5_.w_ref) | copy-start | bytes 11796484
  93.2 7.8 %collective-permute-start.18 = (bf16[256,256]{1,0:T(8,128)(2,1)S(1)}, bf16[256,256]{1,0:T(8,128)(2,1)S(1)}, u32[]{:S(2)}, u32[]{:S(2)}) collective-permute-start(bf16[256,256]{1,0:T(8,128)(2,1)S(1)} %get-tuple-element.29), channel_id=1, source_target_pairs={{8,0},{9,1},{10,2},{11,3},{12,4},{13,5},{14,6},{15,7},{0,8},{1,9},... | collective-permute-start | bytes 393224 | tf_op jit(solution)/shard_map/ppermute | solution.py:39
  101.1 9.5 %collective-permute-start.19 = (bf16[512,256]{1,0:T(8,128)(2,1)S(1)}, bf16[512,256]{1,0:T(8,128)(2,1)S(1)}, u32[]{:S(2)}, u32[]{:S(2)}) collective-permute-start(bf16[512,256]{1,0:T(8,128)(2,1)S(1)} %constant_dynamic-update-slice_fusion.refs_2_), channel_id=1, source_target_pairs={{7,0},{0,1},{1,2},{2,3},{3,4},{4,5},{5,6},{6,7},{15,8},{8,9},{9,10... | collective-permute-start | bytes 786440 | tf_op jit(solution)/shard_map/ppermute | solution.py:39
  102.6 8.3 %collective-permute-start.23 = (bf16[512,256]{1,0:T(8,128)(2,1)S(1)}, bf16[512,256]{1,0:T(8,128)(2,1)S(1)}, u32[]{:S(2)}, u32[]{:S(2)}) collective-permute-start(bf16[512,256]{1,0:T(8,128)(2,1)S(1)} %constant_dynamic-update-slice_fusion.refs_2_), channel_id=1, source_target_pairs={{1,0},{2,1},{3,2},{4,3},{5,4},{6,5},{7,6},{0,7},{9,8},{10,9},{11,1... | collective-permute-start | bytes 786440 | tf_op jit(solution)/shard_map/ppermute | solution.py:39
  110.5 8.5 %collective-permute-start.20 = (bf16[512,256]{1,0:T(8,128)(2,1)S(1)}, bf16[512,256]{1,0:T(8,128)(2,1)S(1)}, u32[]{:S(2)}, u32[]{:S(2)}) collective-permute-start(bf16[512,256]{1,0:T(8,128)(2,1)S(1)} %collective-permute-done.19.refs_2_), channel_id=1, source_target_pairs={{7,0},{0,1},{1,2},{2,3},{3,4},{4,5},{5,6},{6,7},{15,8},{8,9},{9,10... | collective-permute-start | bytes 786440 | tf_op jit(solution)/shard_map/ppermute | solution.py:39
  110.9 8.2 %collective-permute-start.24 = (bf16[512,256]{1,0:T(8,128)(2,1)S(1)}, bf16[512,256]{1,0:T(8,128)(2,1)S(1)}, u32[]{:S(2)}, u32[]{:S(2)}) collective-permute-start(bf16[512,256]{1,0:T(8,128)(2,1)S(1)} %collective-permute-done.23.refs_3_), channel_id=1, source_target_pairs={{1,0},{2,1},{3,2},{4,3},{5,4},{6,5},{7,6},{0,7},{9,8},{10,9},{11,1... | collective-permute-start | bytes 786440 | tf_op jit(solution)/shard_map/ppermute | solution.py:39
  119.1 8.3 %collective-permute-start.21 = (bf16[512,256]{1,0:T(8,128)(2,1)S(1)}, bf16[512,256]{1,0:T(8,128)(2,1)S(1)}, u32[]{:S(2)}, u32[]{:S(2)}) collective-permute-start(bf16[512,256]{1,0:T(8,128)(2,1)S(1)} %collective-permute-done.20.refs_2_), channel_id=1, source_target_pairs={{7,0},{0,1},{1,2},{2,3},{3,4},{4,5},{5,6},{6,7},{15,8},{8,9},{9,10... | collective-permute-start | bytes 786440 | tf_op jit(solution)/shard_map/ppermute | solution.py:39
  119.1 8.4 %collective-permute-start.25 = (bf16[512,256]{1,0:T(8,128)(2,1)S(1)}, bf16[512,256]{1,0:T(8,128)(2,1)S(1)}, u32[]{:S(2)}, u32[]{:S(2)}) collective-permute-start(bf16[512,256]{1,0:T(8,128)(2,1)S(1)} %collective-permute-done.24.refs_3_), channel_id=1, source_target_pairs={{1,0},{2,1},{3,2},{4,3},{5,4},{6,5},{7,6},{0,7},{9,8},{10,9},{11,1... | collective-permute-start | bytes 786440 | tf_op jit(solution)/shard_map/ppermute | solution.py:39
  127.4 8.5 %collective-permute-start.22 = (bf16[256,256]{1,0:T(8,128)(2,1)S(1)}, bf16[256,256]{1,0:T(8,128)(2,1)S(1)}, u32[]{:S(2)}, u32[]{:S(2)}) collective-permute-start(bf16[256,256]{1,0:T(8,128)(2,1)S(1)} %slice.89), channel_id=1, source_target_pairs={{7,0},{0,1},{1,2},{2,3},{3,4},{4,5},{5,6},{6,7},{15,8},{8,9},{9,10... | collective-permute-start | bytes 393224 | tf_op jit(solution)/shard_map/ppermute | solution.py:39
  127.5 8.4 %collective-permute-start.26 = (bf16[256,256]{1,0:T(8,128)(2,1)S(1)}, bf16[256,256]{1,0:T(8,128)(2,1)S(1)}, u32[]{:S(2)}, u32[]{:S(2)}) collective-permute-start(bf16[256,256]{1,0:T(8,128)(2,1)S(1)} %slice.90), channel_id=1, source_target_pairs={{1,0},{2,1},{3,2},{4,3},{5,4},{6,5},{7,6},{0,7},{9,8},{10,9},{11,1... | collective-permute-start | bytes 393224 | tf_op jit(solution)/shard_map/ppermute | solution.py:39
  135.8 4.6 %copy-start.3 = (bf16[256,1536]{1,0:T(8,128)(2,1)S(1)}, bf16[256,1536]{1,0:T(8,128)(2,1)}, u32[]{:S(2)}) copy-start(bf16[256,1536]{1,0:T(8,128)(2,1)} %get-tuple-element.27.tokens_ref) | copy-start | bytes 2359300
  140.4 1.9 %copy-start.2 = (bf16[1024,1536]{1,0:T(8,128)(2,1)S(1)}, bf16[1024,1536]{1,0:T(8,128)(2,1)}, u32[]{:S(2)}) copy-start(bf16[1024,1536]{1,0:T(8,128)(2,1)} %all-gather.5.cloned.1.call-done.w_ref) | copy-start | bytes 9437188
Sparse Core Ops, SparseCore 0:
  10.4 49.5 all-gather.2
  61.9 40.0 all-gather.4
